TPU v7x, 256 devices: a whole 4x4x8 slice. The times are simulated.
256 devices in a mesh: band: 16 (over x, y), sector: 8 (over z), chan: 2 (over core).
Axes of the slice: x: 4, y: 4, z: 8, core: 2. Of those that a mesh axis runs over, the one named last changes fastest.
Arguments:
- obs_features: bfloat16 [131072, 256], P(('band', 'sector')), may hold values from -6 to 6
- obs_owner: int32 [131072, 1], P(('band', 'sector')), may hold values from 0 to 127; in each aligned block of 1024 rows (0 to 1023, 1024 to 2047, ...) at most 12 rows name the same one
- obs_node: int32 [131072], P(('band', 'sector')), may hold values from 0 to 1279
- obs_count: int32 [128], P(('band', 'sector')), may hold values from 3 to 8, as said below
- edge_senders: int32 [983040], P(('band', 'sector')), may hold values from 0 to 4159, as said below
- obs_in_w: bfloat16 [256, 256], replicated, may hold values from -0.375 to 0.375
- obs_in_b: float32 [256], replicated, may hold values from -3 to 3
- obs_out_w: bfloat16 [256, 256], replicated, may hold values from -0.375 to 0.375
- enc_w: bfloat16 [256, 1024], P(None, 'chan'), may hold values from -0.375 to 0.375
- enc_b: float32 [1024], P('chan'), may hold values from -3 to 3
- node_base: bfloat16 [163840, 1024], P(('band', 'sector'), 'chan'), may hold values from -6 to 6
- recv_w: bfloat16 [1024, 1024], P('chan'), may hold values from -0.1875 to 0.1875
- send_w: bfloat16 [1024, 1024], P('chan'), may hold values from -0.1875 to 0.1875
- edge_b: float32 [1024], P('chan'), may hold values from -3 to 3
- channel_scale: float32 [1024], P('chan'), may hold values from 0.25 to 2.75, as said below
- norm_gain: float32 [1024], P('chan'), may hold values from 0.1 to 1.9
Outputs:
- mesh_out: bfloat16 [163840, 1024], P(('band', 'sector'), 'chan')
Inputs may be any that keep to these rules, and one draw needn't show every extreme that they name: `obs_owner`: among the 1024 observations of one device, each owner is named at most 12 times. `obs_count`: some device has all 8 pieces live in every draw. `edge_senders`: values under 1280 name the device's own nodes; larger ones name a boundary node of one of the eight neighbouring blocks; no edge of the first band reads the band before it, none of the last band the band after it, and the centre group is never named. `channel_scale`: positive.
All inputs are finite; a program needn't handle non-finite values.
Results may differ from a plain program's by a relative error of at most 0.0075.
Values may be sent and summed in bfloat16 or wider, within the bound.
A program may use at most 128 MiB of HBM per device.

v0:
```python
import jax
import jax.numpy as jnp
from jax import lax
from jax.sharding import PartitionSpec as P

L = 1024
PIECES = 8
DEGREE = 6


def with_halo(block, sides, width):
    for axis, dim in sides:
        count = lax.axis_size(axis)
        forward = [(i, i + 1) for i in range(count - 1)]
        forward.append((count - 1, 0))
        backward = [(target, source) for source, target in forward]
        low = lax.ppermute(
            lax.slice_in_dim(block, block.shape[dim] - width, None, axis=dim), axis, forward
        )
        high = lax.ppermute(lax.slice_in_dim(block, 0, width, axis=dim), axis, backward)
        block = jnp.concatenate([low, block, high], axis=dim)
    return block


def encode(embedded, enc_w, enc_b):
    return jax.nn.silu(jnp.dot(embedded, enc_w, preferred_element_type=jnp.float32) + enc_b).astype(
        jnp.bfloat16
    )


def local(
    obs_features,
    obs_owner,
    obs_node,
    obs_count,
    edge_senders,
    obs_in_w,
    obs_in_b,
    obs_out_w,
    enc_w,
    enc_b,
    node_base,
    recv_w,
    send_w,
    edge_b,
    channel_scale,
    norm_gain,
):
    band_count = lax.axis_size("band")
    sector_count = lax.axis_size("sector")
    owner_total = band_count * sector_count
    obs_rows = obs_features.shape[0]
    capacity = max(2, obs_rows * 3 // (2 * owner_total))
    node_rows = node_base.shape[0]
    half_width = node_base.shape[1]
    rim_rows = node_rows // 4
    hidden = jax.nn.silu(
        jnp.dot(obs_features, obs_in_w, preferred_element_type=jnp.float32) + obs_in_b
    ).astype(jnp.bfloat16)
    embedded = (
        obs_features.astype(jnp.float32)
        + jnp.dot(hidden, obs_out_w, preferred_element_type=jnp.float32)
    ).astype(jnp.bfloat16)
    owner = obs_owner[:, 0]
    live = jnp.arange(obs_rows, dtype=jnp.int32) < obs_count[0] * (obs_rows // PIECES)
    onehot_owner = (owner[:, None] == jnp.arange(owner_total, dtype=jnp.int32)[None, :]).astype(
        jnp.int32
    )
    position = jnp.sum(jnp.cumsum(onehot_owner, axis=0) * onehot_owner, axis=1) - 1
    target = jnp.where(live, owner * capacity + position, owner_total * capacity)
    slot_ids = (
        jnp.full((owner_total * capacity,), -1, jnp.int32).at[target].set(obs_node, mode="drop")
    )
    content = encode(embedded, enc_w, enc_b)
    payload = (
        jnp.zeros((owner_total * capacity, content.shape[1]), jnp.bfloat16)
        .at[target]
        .set(content, mode="drop")
    )
    arrived, arrived_ids = (
        lax.all_to_all(
            payload.reshape(owner_total, capacity, -1),
            ("band", "sector"),
            split_axis=0,
            concat_axis=0,
            tiled=True,
        ),
        lax.all_to_all(
            slot_ids.reshape(owner_total, capacity),
            ("band", "sector"),
            split_axis=0,
            concat_axis=0,
            tiled=True,
        ),
    )
    arrived = arrived.reshape(owner_total * capacity, -1)
    arrived_ids = arrived_ids.reshape(owner_total * capacity)
    picks = (jnp.arange(node_rows, dtype=jnp.int32)[:, None] == arrived_ids[None, :]).astype(
        jnp.bfloat16
    )
    node_sum = jnp.dot(picks, arrived, preferred_element_type=jnp.float32)
    node_count = jnp.sum(picks, axis=1, dtype=jnp.float32)
    latent = (
        node_base.astype(jnp.float32) + node_sum / jnp.maximum(node_count, 1.0)[:, None]
    ).astype(jnp.bfloat16)
    partial_recv = jnp.dot(latent, recv_w, preferred_element_type=jnp.float32)
    partial_send = jnp.dot(latent, send_w, preferred_element_type=jnp.float32)
    summed_recv, summed_send = (
        lax.psum_scatter(partial_recv, "chan", scatter_dimension=1, tiled=True),
        lax.psum_scatter(partial_send, "chan", scatter_dimension=1, tiled=True),
    )
    recv_proj = summed_recv.astype(jnp.bfloat16)
    send_proj = summed_send.astype(jnp.bfloat16)
    rim = send_proj[:rim_rows].reshape(1, 1, rim_rows, half_width)
    beside_all = with_halo(rim, (("band", 0), ("sector", 1)), 1)
    table = jnp.concatenate([send_proj, beside_all.reshape(9 * rim_rows, half_width)], axis=0)
    sender_rows = table[edge_senders].astype(jnp.float32).reshape(node_rows, DEGREE, half_width)
    base = recv_proj.astype(jnp.float32) + edge_b
    agg = jnp.sum(jax.nn.silu(sender_rows + base[:, None, :]), axis=1)
    scaled = agg * channel_scale
    square_sum = lax.psum(jnp.sum(scaled * scaled, axis=1), "chan")
    normed = scaled * lax.rsqrt(square_sum / L + 1e-05)[:, None] * norm_gain
    return (latent.astype(jnp.float32) + normed).astype(jnp.bfloat16)


def solution(mesh):
    in_specs = (
        P(("band", "sector"), None),
        P(("band", "sector"), None),
        P(("band", "sector")),
        P(("band", "sector")),
        P(("band", "sector")),
        P(),
        P(),
        P(),
        P(None, "chan"),
        P("chan"),
        P(("band", "sector"), "chan"),
        P("chan", None),
        P("chan", None),
        P("chan"),
        P("chan"),
        P("chan"),
    )
    out_specs = P(("band", "sector"), "chan")
    return jax.shard_map(local, mesh=mesh, in_specs=in_specs, out_specs=out_specs, check_vma=False)
```

profile of v0, /device:TPU:1, one launch (start us, length us, event | category | flops | bytes accessed | tf_op | source)
XLA Modules:
  0.0 242.7 jit_solution(14378169714616583793)
XLA Ops:
  6.5 0.9 copy.23
  8.9 4.5 %scatter_custom_fusion = s32[1536]{0:T(1024)S(1)} fusion(s32[1024]{0:T(1024)S(1)} %bitcast.31, s32[1024]{0:T(1024)} %param.18, s32[]{:T(128)} %constant.11.clone.1), kind=kCustom, calls=%fused_computation.42 | custom fusion | bytes 6656 | tf_op jit(solution)/shard_map/scatter | solution.py:72
  14.1 16.3 %all-to-all-start = ((s32[128,1,12]{2,1,0:T(1,128)}), s32[128,1,12]{2,1,0:T(1,128)S(1)}, u32[]{:S(2)}, u32[]{:S(2)}) async-start(s32[128,1,12]{2,1,0:T(1,128)} %bitcast.8), calls=%async_computation | async-start | bytes 131072 | tf_op jit(solution)/shard_map/all_to_all | solution.py:88
  31.5 1.8 multiply_convert_fusion
  33.3 6.0 %scatter_custom_fusion.1 = bf16[1536,512]{1,0:T(8,128)(2,1)S(1)} fusion(s32[1024]{0:T(1024)S(1)} %bitcast.32, bf16[1024,512]{1,0:T(8,128)(2,1)} %multiply_convert_fusion, bf16[]{:T(256)} %constant.9.clone.1), kind=kCustom, calls=%fused_computation.24 | custom fusion | bytes 1573376 | tf_op jit(solution)/shard_map/scatter | solution.py:78
  39.4 1.5 reshape.67
  41.0 13.1 %all-to-all-start.1 = ((bf16[128,12,512]{2,1,0:T(8,128)(2,1)}), bf16[128,12,512]{2,1,0:T(8,128)(2,1)S(1)}, u32[]{:S(2)}, u32[]{:S(2)}) async-start(bf16[128,12,512]{2,1,0:T(8,128)(2,1)} %reshape.67), calls=%async_computation.1 | async-start | bytes 4194304 | tf_op jit(solution)/shard_map/all_to_all | solution.py:81
  55.8 0.9 convert_reduce_fusion
  56.7 49.9 %all-to-all-done.1 = bf16[128,12,512]{2,1,0:T(8,128)(2,1)S(1)} async-done(((bf16[128,12,512]{2,1,0:T(8,128)(2,1)}), bf16[128,12,512]{2,1,0:T(8,128)(2,1)S(1)}, u32[]{:S(2)}, u32[]{:S(2)}) %all-to-all-start.1) | async-done | bytes 1572896 | tf_op jit(solution)/shard_map/all_to_all | solution.py:81
  106.6 1.3 reshape.68
  108.0 4.1 %fusion.5 = bf16[1280,512]{1,0:T(8,128)(2,1)S(1)} fusion(bf16[1536,512]{1,0:T(8,128)(2,1)} %reshape.68, s32[1536]{0:T(1024)S(1)} %eq.49, bf16[1280,512]{1,0:T(8,128)(2,1)} %param.26, f32[1280]{0:T(1024)S(1)} %broadcast_maximum_fusion), kind=kOutput, calls=%fused_computation.12 | convolution fusion | flops 2017853440 | bytes 4205568 | tf_op jit(solution)/shard_map/dot_general | solution.py:101
  112.1 3.9 %fusion.16 = f32[1280,1024]{1,0:T(8,128)} fusion(bf16[1280,512]{1,0:T(8,128)(2,1)S(1)} %fusion.5, bf16[512,1024]{1,0:T(8,128)(2,1)S(1)} %copy-done), kind=kOutput, calls=%fused_computation.45 | convolution fusion | flops 1342177280 | bytes 7602176 | tf_op jit(solution)/shard_map/dot_general | solution.py:107
  116.1 1.1 copy-done.10
  117.2 3.8 %fusion.17 = f32[1280,1024]{1,0:T(8,128)} fusion(bf16[1280,512]{1,0:T(8,128)(2,1)S(1)} %fusion.5, bf16[512,1024]{1,0:T(8,128)(2,1)S(1)} %copy-done.10), kind=kOutput, calls=%fused_computation.46 | convolution fusion | flops 1342177280 | bytes 7602176 | tf_op jit(solution)/shard_map/dot_general | solution.py:106
  121.1 8.8 %reduce-scatter.3.cloned.1.call-done = f32[1280,512]{1,0:T(8,128)} async-done(((f32[1280,1024]{1,0:T(8,128)}), f32[1280,512]{1,0:T(8,128)}) %reduce-scatter.3.cloned.1.call-update) | async-done | bytes 2621456 | tf_op jit(solution)/shard_map/reduce_scatter | solution.py:110
  129.9 1.9 convert_element_type.61
  131.9 1.1 collective-permute-start
  133.0 3.8 %collective-permute-start.1 = (bf16[1,1,320,512]{3,2,1,0:T(8,128)(2,1)S(1)}, bf16[1,1,320,512]{3,2,1,0:T(8,128)(2,1)S(1)}, u32[]{:S(2)}, u32[]{:S(2)}) collective-permute-start(bf16[1,1,320,512]{3,2,1,0:T(8,128)(2,1)S(1)} %slice_bitcast_fusion), channel_id=1, source_target_pairs={{16,0},{32,16},{48,32},{64,48},{80,64},{96,80},{112,96},{128,112},... | collective-permute-start | bytes 983048 | tf_op jit(solution)/shard_map/ppermute | solution.py:20
  136.7 7.9 %collective-permute-done = bf16[1,1,320,512]{3,2,1,0:T(8,128)(2,1)S(1)} collective-permute-done((bf16[1,1,320,512]{3,2,1,0:T(8,128)(2,1)S(1)}, bf16[1,1,320,512]{3,2,1,0:T(8,128)(2,1)S(1)}, u32[]{:S(2)}, u32[]{:S(2)}) %collective-permute-start) | collective-permute-done | bytes 327712 | tf_op jit(solution)/shard_map/ppermute | solution.py:17
  144.7 1.1 pad_maximum_fusion.2
  146.5 2.0 collective-permute-start.3
  148.5 4.1 %reduce-scatter.5.cloned.1.call-done = f32[1280,512]{1,0:T(8,128)} async-done(((f32[1280,1024]{1,0:T(8,128)}), f32[1280,512]{1,0:T(8,128)}) %reduce-scatter.5.cloned.1.call-update) | async-done | bytes 2621456 | tf_op jit(solution)/shard_map/reduce_scatter | solution.py:109
  152.6 3.6 %convert_add_fusion = f32[1280,512]{1,0:T(8,128)} fusion(f32[512]{0:T(512)S(1)} %copy-done.8, f32[1280,512]{1,0:T(8,128)} %reduce-scatter.5.cloned.1.call-done), kind=kLoop, calls=%fused_computation.16 | loop fusion | flops 1966080 | bytes 5244928 | tf_op jit(solution)/shard_map/add | solution.py:118
  156.2 13.5 %collective-permute-done.2 = bf16[3,1,320,512]{3,2,1,0:T(8,128)(2,1)S(1)} collective-permute-done((bf16[3,1,320,512]{3,2,1,0:T(8,128)(2,1)}, bf16[3,1,320,512]{3,2,1,0:T(8,128)(2,1)S(1)}, u32[]{:S(2)}, u32[]{:S(2)}) %collective-permute-start.2) | collective-permute-done | bytes 983072 | tf_op jit(solution)/shard_map/ppermute | solution.py:17
  169.7 1.4 pad_maximum_fusion.1
  171.1 2.2 pad_maximum_fusion
  173.4 25.3 %gather_fusion = bf16[7680,512]{1,0:T(8,128)(2,1)} fusion(bf16[4160,512]{1,0:T(8,128)(2,1)} %pad_maximum_fusion, s32[8192]{0:T(1024)S(1)} %pad_clamp_fusion), kind=kCustom, calls=%fused_computation | custom fusion | bytes 15759360 | tf_op jit(solution)/shard_map/gather | solution.py:117
  198.6 14.7 %reshape.71 = f32[1280,6,512]{2,1,0:T(8,128)} reshape(bf16[7680,512]{1,0:T(8,128)(2,1)} %gather_fusion) | data formatting | bytes 23592960 | tf_op jit(solution)/shard_map/convert_element_type | solution.py:117
  213.4 13.3 %multiply_reduce_fusion = f32[1280,512]{1,0:T(8,128)S(1)} fusion(f32[1280,6,512]{2,1,0:T(8,128)} %reshape.71, f32[1280,512]{1,0:T(8,128)} %convert_add_fusion), kind=kLoop, calls=%fused_computation.3 | loop fusion | flops 22937600 | bytes 20971520 | tf_op jit(solution)/shard_map/reduce_sum | solution.py:119
  226.6 1.5 copy-done.2
  228.5 3.9 %psum.7 = f32[1280]{0:T(1024)S(1)} all-reduce(f32[1280]{0:T(1024)S(1)} %multiply_reduce_fusion.1), channel_id=1, replica_groups=mesh['band'=16,'sector'=8,'chan'=2] {'chan'}, use_global_device_ids=true, to_apply=%region_10.11 | all-reduce | flops 1280 | bytes 10240 | tf_op jit(solution)/shard_map/psum | solution.py:121
  232.4 3.4 %add_convert_fusion = bf16[1280,512]{1,0:T(8,128)(2,1)} fusion(bf16[1280,512]{1,0:T(8,128)(2,1)S(1)} %copy-done.4, f32[1280,512]{1,0:T(8,128)} %copy-done.2, f32[512]{0:T(512)S(1)} %copy-done.9, f32[1280]{0:T(1024)S(1)} %add_rsqrt_fusion, f32[512]{0:T(512)S(1)} %copy-done.7), kind=kLoop, calls=%fused_computation.14 | loop fusion | flops 3932160 | bytes 5252096 | tf_op jit(solution)/shard_map/convert_element_type | solution.py:123
  (60 shorter events, 5.4 us)
Async XLA Ops:
  6.5 105.6 %copy-start = (bf16[512,1024]{1,0:T(8,128)(2,1)S(1)}, bf16[512,1024]{1,0:T(8,128)(2,1)}, u32[]{:S(2)}) copy-start(bf16[512,1024]{1,0:T(8,128)(2,1)} %param.28) | copy-start | bytes 3145732
  6.5 1.3 copy-start.5
  6.5 23.9 %copy-start.11 = (bf16[1024,256]{1,0:T(8,128)(2,1)S(1)}, bf16[1024,256]{1,0:T(8,128)(2,1)}, u32[]{:S(2)}) copy-start(bf16[1024,256]{1,0:T(8,128)(2,1)} %param.16) | copy-start | bytes 1572868
  6.5 23.9 %copy-start.13 = (bf16[256,256]{1,0:T(8,128)(2,1)S(1)}, bf16[256,256]{1,0:T(8,128)(2,1)}, u32[]{:S(2)}) copy-start(bf16[256,256]{1,0:T(8,128)(2,1)} %param.21) | copy-start | bytes 393220
  6.5 24.0 %copy-start.16 = (f32[256]{0:T(256)S(1)}, f32[256]{0:T(256)}, u32[]{:S(2)}) copy-start(f32[256]{0:T(256)} %param.22) | copy-start | bytes 3076
  14.1 26.9 %all-to-all-start = ((s32[128,1,12]{2,1,0:T(1,128)}), s32[128,1,12]{2,1,0:T(1,128)S(1)}, u32[]{:S(2)}, u32[]{:S(2)}) async-start(s32[128,1,12]{2,1,0:T(1,128)} %bitcast.8), calls=%async_computation | async-start | bytes 131072 | tf_op jit(solution)/shard_map/all_to_all | solution.py:88
  30.5 1.0 copy-start.12
  30.5 1.0 copy-start.14
  30.5 1.0 copy-start.15
  41.0 65.6 %all-to-all-start.1 = ((bf16[128,12,512]{2,1,0:T(8,128)(2,1)}), bf16[128,12,512]{2,1,0:T(8,128)(2,1)S(1)}, u32[]{:S(2)}, u32[]{:S(2)}) async-start(bf16[128,12,512]{2,1,0:T(8,128)(2,1)} %reshape.67), calls=%async_computation.1 | async-start | bytes 4194304 | tf_op jit(solution)/shard_map/all_to_all | solution.py:81
  54.2 75.7 %reduce-scatter.3.cloned.1.call-start = ((), (), s32[]{:S(2)}) async-start(), calls=%async_computation.4 | async-start | bytes 7864320 | tf_op jit(solution)/shard_map/reduce_scatter | solution.py:110
  112.1 4.0 %copy-start.3 = (bf16[1280,512]{1,0:T(8,128)(2,1)}, bf16[1280,512]{1,0:T(8,128)(2,1)S(1)}, u32[]{:S(2)}) copy-start(bf16[1280,512]{1,0:T(8,128)(2,1)S(1)} %fusion.5) | copy-start | bytes 3932164
  116.0 1.2 copy-start.10
  116.0 36.6 %reduce-scatter.5.cloned.1.call-start = ((), (), s32[]{:S(2)}) async-start(), calls=%async_computation.5 | async-start | bytes 7864320 | tf_op jit(solution)/shard_map/reduce_scatter | solution.py:109
  121.1 27.4 %copy-start.6 = (s32[7680]{0:T(1024)S(1)}, s32[7680]{0:T(1024)}, u32[]{:S(2)}) copy-start(s32[7680]{0:T(1024)} %param.20) | copy-start | bytes 92164
  121.1 31.5 %copy-start.8 = (f32[512]{0:T(512)S(1)}, f32[512]{0:T(512)}, u32[]{:S(2)}) copy-start(f32[512]{0:T(512)} %param.29) | copy-start | bytes 6148
  131.9 12.8 %collective-permute-start = (bf16[1,1,320,512]{3,2,1,0:T(8,128)(2,1)S(1)}, bf16[1,1,320,512]{3,2,1,0:T(8,128)(2,1)S(1)}, u32[]{:S(2)}, u32[]{:S(2)}) collective-permute-start(bf16[1,1,320,512]{3,2,1,0:T(8,128)(2,1)S(1)} %slice_bitcast_fusion), channel_id=1, source_target_pairs={{0,16},{16,32},{32,48},{48,64},{64,80},{80,96},{96,112},{112,128},... | collective-permute-start | bytes 983048 | tf_op jit(solution)/shard_map/ppermute | solution.py:17
  133.0 11.7 %collective-permute-start.1 = (bf16[1,1,320,512]{3,2,1,0:T(8,128)(2,1)S(1)}, bf16[1,1,320,512]{3,2,1,0:T(8,128)(2,1)S(1)}, u32[]{:S(2)}, u32[]{:S(2)}) collective-permute-start(bf16[1,1,320,512]{3,2,1,0:T(8,128)(2,1)S(1)} %slice_bitcast_fusion), channel_id=1, source_target_pairs={{16,0},{32,16},{48,32},{64,48},{80,64},{96,80},{112,96},{128,112},... | collective-permute-start | bytes 983048 | tf_op jit(solution)/shard_map/ppermute | solution.py:20
  145.7 24.0 %collective-permute-start.2 = (bf16[3,1,320,512]{3,2,1,0:T(8,128)(2,1)}, bf16[3,1,320,512]{3,2,1,0:T(8,128)(2,1)S(1)}, u32[]{:S(2)}, u32[]{:S(2)}) collective-permute-start(bf16[3,1,320,512]{3,2,1,0:T(8,128)(2,1)} %pad_maximum_fusion.2), channel_id=1, source_target_pairs={{0,2},{2,4},{4,6},{6,8},{8,10},{10,12},{12,14},{14,0},{1,3},{3,5},... | collective-permute-start | bytes 2949128 | tf_op jit(solution)/shard_map/ppermute | solution.py:17
  146.5 23.2 %collective-permute-start.3 = (bf16[3,1,320,512]{3,2,1,0:T(8,128)(2,1)}, bf16[3,1,320,512]{3,2,1,0:T(8,128)(2,1)}, u32[]{:S(2)}, u32[]{:S(2)}) collective-permute-start(bf16[3,1,320,512]{3,2,1,0:T(8,128)(2,1)} %pad_maximum_fusion.2), channel_id=1, source_target_pairs={{2,0},{4,2},{6,4},{8,6},{10,8},{12,10},{14,12},{0,14},{3,1},{5,3},... | collective-permute-start | bytes 2949128 | tf_op jit(solution)/shard_map/ppermute | solution.py:20
  213.4 14.8 %copy-start.7 = (f32[512]{0:T(512)S(1)}, f32[512]{0:T(512)}, u32[]{:S(2)}) copy-start(f32[512]{0:T(512)} %param.30) | copy-start | bytes 6148
  226.6 1.5 copy-start.2
  228.1 4.3 %copy-start.4 = (bf16[1280,512]{1,0:T(8,128)(2,1)S(1)}, bf16[1280,512]{1,0:T(8,128)(2,1)}, u32[]{:S(2)}) copy-start(bf16[1280,512]{1,0:T(8,128)(2,1)} %copy-done.3) | copy-start | bytes 3932164
  228.1 4.3 %copy-start.9 = (f32[512]{0:T(512)S(1)}, f32[512]{0:T(512)}, u32[]{:S(2)}) copy-start(f32[512]{0:T(512)} %param.31) | copy-start | bytes 6148
  232.4 3.4 %copy-start.1 = (bf16[512,1024]{1,0:T(8,128)(2,1)S(1)}, bf16[512,1024]{1,0:T(8,128)(2,1)}, u32[]{:S(2)}) copy-start(bf16[512,1024]{1,0:T(8,128)(2,1)} %param.28) | copy-start | bytes 3145732
Sparse Core Ops, SparseCore 0:
  116.1 13.7 reduce-scatter.2
  132.7 19.8 reduce-scatter.4
where the time goes:
time: 244 us; the launch traced here: 243 us
  waiting for transfers between devices  84.4 us (35%)
  local copies, waits for them, and re-layouts  59 us (24%)
  starting transfers between devices  37.3 us (15%)
  other arithmetic  29.6 us (12%)
  between operations  14.4 us (6%)
  matrix products  14.1 us (6%)
  blocking collectives  3.92 us (2%)
    all_to_all x1, waiting for transfers between devices, local(): lax.all_to_all(payload.reshape(owner_total, capacity, -1), ('band', 'sect...  49.9 us
    gather x1, local copies, waits for them, and re-layouts, local(): table[edge_senders].astype(jnp.float32)  25.3 us
    ppermute x2, waiting for transfers between devices, with_halo(): lax.ppermute(lax.slice_in_dim(block, block.shape[dim] - width, None, axis...  21.4 us
    all_to_all x1, starting transfers between devices, local(): lax.all_to_all(slot_ids.reshape(owner_total, capacity), ('band', 'sector'...  16.3 us
    convert_element_type x1, local copies, waits for them, and re-layouts, local(): table[edge_senders].astype(jnp.float32)  14.7 us
    reduce_sum x1, other arithmetic, local(): agg = jnp.sum(jax.nn.silu(sender_rows + base[:, None, :]), axis=1)  13.3 us
    all_to_all x1, starting transfers between devices, local(): lax.all_to_all(payload.reshape(owner_total, capacity, -1), ('band', 'sect...  13.1 us
    reduce_scatter x1, waiting for transfers between devices, local(): lax.psum_scatter(partial_send, 'chan', scatter_dimension=1, tiled=True)  8.84 us
  transfers between devices with their start and end apart: 8, of which 6 were waited for; matrix products, arithmetic and copies ran while one was open for 9% of the time, Pallas kernels for 0%

commit v1 on v0

v1 whole, which is shorter than its diff:
```python
import functools

import jax
import jax.numpy as jnp
from jax import lax
from jax.experimental import pallas as pl
from jax.experimental.pallas import tpu as pltpu
from jax.sharding import PartitionSpec as P

PIECES = 8
DEGREE = 6
SLOTS = 16
ID_ROW = 12
GROUP = 8
LANES = 128
LOW = 64
PAD = 8
MESH = pl.DeviceIdType.MESH
F32 = jnp.float32
BF16 = jnp.bfloat16
STEP_ROWS = 256


def dot(a, b):
    return jnp.dot(a, b, preferred_element_type=F32)


def iota(shape, axis):
    return lax.broadcasted_iota(jnp.int32, shape, axis)


def half_silu(h):
    return h + h * jnp.tanh(h)


def kernel(
    bands,
    sectors,
    owner_ref,
    node_ref,
    count_ref,
    index_ref,
    obs_ref,
    in_w_ref,
    in_b_ref,
    out_w_ref,
    enc_w_ref,
    enc_b_ref,
    base_hbm,
    recv_hbm,
    send_hbm,
    edge_b_ref,
    scale_ref,
    gain_ref,
    out_hbm,
    send_buf,
    arrived,
    message,
    node_base,
    recv_w,
    send_w,
    picks,
    latent,
    table,
    recv_base,
    rim,
    halo,
    agg,
    part,
    part_in,
    out_buf,
    local_sem,
    weight_sem,
    weight_in_sem,
    send_sem,
    arrive_sem,
    pass_sem,
    pass_in_sem,
    latent_sem,
    latent_in_sem,
    halo_sem,
    halo_in_sem,
    part_sem,
    part_in_sem,
    out_sem,
):
    band = lax.axis_index("band")
    sector = lax.axis_index("sector")
    core = lax.axis_index("chan")
    other = 1 - core
    geo = bands * sectors
    pairs = geo // 2
    me = band * sectors + sector
    my_pair = me // 2
    parity = (me + core) % 2
    partner = (band, sector, other)
    rows = obs_ref.shape[0]
    node_rows, width = latent.shape[1:]
    tiles = width // LANES
    rim_rows = node_rows // 4
    groups = 2 * pairs // GROUP

    def device_of(block, core_of):
        return (block // sectors, block % sectors, core_of)

    def target_of(k):
        return 2 * ((my_pair + 1 + k) % pairs) + parity

    around = [(i, j) for i in (-1, 0, 1) for j in (-1, 0, 1) if (i, j) != (0, 0)]

    def neighbour(i, j):
        return ((band + i + bands) % bands, (sector + j + sectors) % sectors, core)

    local = [
        pltpu.make_async_copy(
            recv_hbm.at[:, pl.ds(pl.multiple_of(core * width, width), width)],
            recv_w.at[core],
            local_sem.at[0],
        ),
        pltpu.make_async_copy(
            send_hbm.at[:, pl.ds(pl.multiple_of(core * width, width), width)],
            send_w.at[core],
            local_sem.at[1],
        ),
        pltpu.make_async_copy(base_hbm, node_base, local_sem.at[2]),
    ]
    for copy in local:
        copy.start()

    barrier = pltpu.get_barrier_semaphore()

    def greet(k, carry):
        target = target_of(k)

        @pl.when(target != me)
        def _():
            pl.semaphore_signal(
                barrier, inc=1, device_id=device_of(target, core), device_id_type=MESH
            )

        return carry

    lax.fori_loop(0, pairs, greet, 0)
    for i, j in around:
        pl.semaphore_signal(barrier, inc=1, device_id=neighbour(i, j), device_id_type=MESH)
    pl.semaphore_signal(barrier, inc=1, device_id=partner, device_id_type=MESH)

    obs = obs_ref[...]
    hidden = half_silu(0.5 * (dot(obs, in_w_ref[...]) + in_b_ref[...])).astype(BF16)
    embedded = (obs.astype(F32) + dot(hidden, out_w_ref[...])).astype(BF16)
    owner = owner_ref[...]
    node = node_ref[...]
    live = iota((1, rows), 1) < count_ref[0] * (rows // PIECES)
    same = owner == iota((geo, rows), 0)
    upto = (iota((rows, rows), 0) <= iota((rows, rows), 1)).astype(F32).astype(BF16)
    ranks = dot(same.astype(F32).astype(BF16), upto)
    position = jnp.sum(jnp.where(same, ranks, 0.0), axis=0, keepdims=True).astype(jnp.int32) - 1
    pair = owner // 2
    valid = jnp.logical_and(live, owner % 2 == parity)
    step = (pair - my_pair - 1 + 2 * pairs) % pairs
    slot = jnp.where(valid, step * SLOTS + position, -1)
    lane = SLOTS * (step % GROUP) + position
    high = iota((2 * LANES, rows), 0) == lane
    low = iota((2 * LANES, rows), 0) == lane + LANES
    ids = jnp.where(
        high,
        (node // LOW + 1).astype(F32),
        jnp.where(low, (node % LOW).astype(F32), 0.0),
    ).astype(BF16)
    mine = (iota((pairs, rows), 0) == jnp.where(valid, step, -1)).astype(F32).astype(BF16)
    id_rows = lax.dot_general(
        mine, ids, (((1,), (1,)), ((), ())), preferred_element_type=F32
    ).astype(BF16)

    pl.semaphore_wait(barrier, pairs - 1 + core + len(around) + 1)

    weights = [
        pltpu.make_async_remote_copy(
            src_ref=source.at[:, pl.ds(pl.multiple_of(other * width, width), width)],
            dst_ref=target.at[core],
            send_sem=weight_sem.at[n],
            recv_sem=weight_in_sem.at[n],
            device_id=partner,
            device_id_type=MESH,
        )
        for n, (source, target) in enumerate(((send_hbm, send_w), (recv_hbm, recv_w)))
    ]

    def block_copy(k):
        return pltpu.make_async_remote_copy(
            src_ref=send_buf.at[k],
            dst_ref=arrived.at[core, k],
            send_sem=send_sem.at[k],
            recv_sem=arrive_sem.at[k],
            device_id=device_of(target_of(k), core),
            device_id_type=MESH,
        )

    def own_copy(k):
        return pltpu.make_async_copy(send_buf.at[k], arrived.at[core, k], local_sem.at[3])

    per_step = STEP_ROWS // SLOTS

    def pack(step_index, carry):
        first = pl.multiple_of(step_index * STEP_ROWS, STEP_ROWS)
        place = (slot == first + iota((STEP_ROWS, rows), 0)).astype(F32).astype(BF16)
        spread = (
            first + iota((STEP_ROWS, pairs), 0) == iota((STEP_ROWS, pairs), 1) * SLOTS + ID_ROW
        )
        block = dot(place, embedded) + dot(spread.astype(F32).astype(BF16), id_rows)
        send_buf[pl.ds(step_index * per_step, per_step)] = block.astype(BF16).reshape(
            per_step, SLOTS, -1
        )

        def send(n, inner):
            k = step_index * per_step + n

            @pl.when(target_of(k) != me)
            def _():
                block_copy(k).start()

            @pl.when(target_of(k) == me)
            def _():
                own_copy(k).start()

            return inner

        lax.fori_loop(0, per_step, send, 0)
        return carry

    lax.fori_loop(0, pairs // per_step, pack, 0)
    for copy in weights:
        copy.start()

    def pass_on(g, side):
        block = arrived.at[side, pl.ds(g * per_step, per_step)]
        return pltpu.make_async_remote_copy(
            src_ref=block,
            dst_ref=block,
            send_sem=pass_sem.at[g],
            recv_sem=pass_in_sem.at[g],
            device_id=partner,
            device_id_type=MESH,
        )

    def encode(side, g):
        block = arrived[side, pl.ds(g * per_step, per_step)].reshape(STEP_ROWS, -1)
        content = half_silu(0.5 * (dot(block, enc_w_ref[...]) + enc_b_ref[...])).astype(BF16)
        first = pl.multiple_of(side * (pairs * SLOTS) + g * STEP_ROWS, STEP_ROWS)
        message[pl.ds(first, STEP_ROWS), :] = content

    def receive(g, carry):
        def arrive(n, inner):
            k = g * per_step + n

            @pl.when(target_of(k) != me)
            def _():
                block_copy(k).wait_recv()

            @pl.when(target_of(k) == me)
            def _():
                own_copy(k).wait()

            return inner

        lax.fori_loop(0, per_step, arrive, 0)
        pass_on(g, core).start()
        encode(core, g)
        return carry

    lax.fori_loop(0, pairs // per_step, receive, 0)

    def receive_passed(g, carry):
        pass_on(g, other).wait_recv()
        encode(other, g)
        return carry

    lax.fori_loop(0, pairs // per_step, receive_passed, 0)

    slots = 2 * pairs * SLOTS
    at = iota((groups, slots), 1)
    chosen = jnp.logical_and(
        at // (GROUP * SLOTS) == iota((groups, slots), 0), at % SLOTS == ID_ROW
    )
    found = dot(chosen.astype(F32).astype(BF16), arrived[...].reshape(slots, -1))
    slot_ids = ((found[:, :LANES] - 1.0) * LOW + found[:, LANES:]).astype(jnp.int32)

    def rows_of(q):
        return pl.ds(pl.multiple_of(q * rim_rows, rim_rows), rim_rows)

    def latent_copy(q, side):
        block = latent.at[side, rows_of(q)]
        return pltpu.make_async_remote_copy(
            src_ref=block,
            dst_ref=block,
            send_sem=latent_sem.at[q],
            recv_sem=latent_in_sem.at[q],
            device_id=partner,
            device_id_type=MESH,
        )

    def make_latent(q):
        names = iota((rim_rows, LANES), 0) + q * rim_rows
        count = jnp.zeros((rim_rows, LANES), F32)
        for g in range(groups):
            hit = (names == slot_ids[g : g + 1, :]).astype(F32)
            count = count + hit
            picks[:, g * LANES : (g + 1) * LANES] = hit.astype(BF16)
        total = dot(picks[...], message[...])
        scale = 1.0 / jnp.maximum(jnp.sum(count, axis=1, keepdims=True), 1.0)
        latent[core, rows_of(q)] = (
            node_base[rows_of(q), :].astype(F32) + total * scale
        ).astype(BF16)
        latent_copy(q, core).start()

    def project(q, weight):
        return dot(latent[0, rows_of(q)], weight[0]) + dot(latent[1, rows_of(q)], weight[1])

    def project_send(q):
        value = 0.5 * project(q, send_w).astype(BF16).astype(F32)
        for t in range(tiles):
            table[pl.ds(PAD + q * (rim_rows * tiles) + t, rim_rows, stride=tiles), :] = value[
                :, t * LANES : (t + 1) * LANES
            ]

    def project_recv(q):
        value = 0.5 * (project(q, recv_w).astype(BF16).astype(F32) + edge_b_ref[...])
        for t in range(tiles):
            recv_base[pl.ds(q * (rim_rows * tiles) + t, rim_rows, stride=tiles), :] = value[
                :, t * LANES : (t + 1) * LANES
            ]

    local[2].wait()
    make_latent(0)
    local[1].wait()
    weights[0].wait_recv()
    latent_copy(0, other).wait_recv()
    project_send(0)
    rim[...] = table[pl.ds(PAD, rim_rows * tiles), :].astype(BF16)

    def halo_copy(n):
        i, j = around[n]
        return pltpu.make_async_remote_copy(
            src_ref=rim,
            dst_ref=halo.at[(1 - i) * 3 + 1 - j],
            send_sem=halo_sem.at[n],
            recv_sem=halo_in_sem.at[n],
            device_id=neighbour(i, j),
            device_id_type=MESH,
        )

    for n in range(len(around)):
        halo_copy(n).start()

    def later_latent(q, carry):
        make_latent(q)
        return carry

    lax.fori_loop(1, 4, later_latent, 0)
    local[0].wait()
    weights[1].wait_recv()
    project_recv(0)

    def later_project(q, carry):
        latent_copy(q, other).wait_recv()
        project_send(q)
        project_recv(q)
        return carry

    lax.fori_loop(1, 4, later_project, 0)

    for n, (i, j) in enumerate(around):
        halo_copy(n).wait_recv()
        group = (1 - i) * 3 + 1 - j
        first = PAD + (node_rows + group * rim_rows) * tiles
        table[pl.ds(first, rim_rows * tiles), :] = halo[group].astype(F32)

    upper = iota((2 * tiles, LANES), 0) < tiles

    def two_nodes(m):
        base = recv_base[pl.ds(pl.multiple_of(m * 2 * tiles, 2 * tiles), 2 * tiles), :]
        total = None
        for k in range(DEGREE):
            even = index_ref[2 * DEGREE * m + k]
            odd = index_ref[2 * DEGREE * m + DEGREE + k]
            sender = jnp.where(
                upper, table[pl.ds(even, 2 * tiles), :], table[pl.ds(odd, 2 * tiles), :]
            )
            term = half_silu(base + sender)
            total = term if total is None else total + term
        agg[pl.ds(pl.multiple_of(m * 2 * tiles, 2 * tiles), 2 * tiles), :] = total

    chunk = part.shape[1]
    chunks = node_rows // chunk
    unroll = 8

    def part_copy(n):
        return pltpu.make_async_remote_copy(
            src_ref=part.at[n],
            dst_ref=part_in.at[n],
            send_sem=part_sem.at[n],
            recv_sem=part_in_sem.at[n],
            device_id=partner,
            device_id_type=MESH,
        )

    def out_copy(n):
        span = pl.ds(pl.multiple_of(n * chunk, chunk), chunk)
        return pltpu.make_async_copy(out_buf.at[span], out_hbm.at[span], out_sem.at[n])

    def scaled(n, t):
        return (
            agg[pl.ds(n * (chunk * tiles) + t, chunk, stride=tiles), :]
            * scale_ref[:, t * LANES : (t + 1) * LANES]
        )

    def edges(n, carry):
        def some(m, inner):
            for u in range(unroll):
                two_nodes(n * (chunk // 2) + m * unroll + u)
            return inner

        lax.fori_loop(0, chunk // 2 // unroll, some, 0)
        square = jnp.zeros((chunk, LANES), F32)
        for t in range(tiles):
            value = scaled(n, t)
            square = square + value * value
        part[n] = square
        part_copy(n).start()
        return carry

    def finish(n, carry):
        part_copy(n).wait_recv()
        mean = jnp.sum(part[n] + part_in[n], axis=1, keepdims=True) / (2 * width)
        factor = lax.rsqrt(mean + 1e-05)
        span = pl.ds(pl.multiple_of(n * chunk, chunk), chunk)
        for t in range(tiles):
            lanes = slice(t * LANES, (t + 1) * LANES)
            normed = scaled(n, t) * factor * gain_ref[:, lanes]
            out_buf[span, lanes] = (latent[core, span, lanes].astype(F32) + normed).astype(BF16)
        out_copy(n).start()
        return carry

    def edges_and_finish(n, carry):
        edges(n, carry)
        return finish(n - 1, carry)

    edges(0, 0)
    lax.fori_loop(1, chunks, edges_and_finish, 0)
    finish(chunks - 1, 0)

    def drain_blocks(k, carry):
        @pl.when(target_of(k) != me)
        def _():
            block_copy(k).wait_send()

        return carry

    lax.fori_loop(0, pairs, drain_blocks, 0)

    def drain_passed(g, carry):
        pass_on(g, core).wait_send()
        return carry

    lax.fori_loop(0, pairs // per_step, drain_passed, 0)
    for copy in weights:
        copy.wait_send()
    for q in range(4):
        latent_copy(q, core).wait_send()
    for n in range(len(around)):
        halo_copy(n).wait_send()
    for n in range(chunks):
        part_copy(n).wait_send()
        out_copy(n).wait()


def local(
    obs_features,
    obs_owner,
    obs_node,
    obs_count,
    edge_senders,
    obs_in_w,
    obs_in_b,
    obs_out_w,
    enc_w,
    enc_b,
    node_base,
    recv_w,
    send_w,
    edge_b,
    channel_scale,
    norm_gain,
):
    bands = lax.axis_size("band")
    sectors = lax.axis_size("sector")
    geo = bands * sectors
    pairs = geo // 2
    rows, embed = obs_features.shape
    node_rows, width = node_base.shape
    tiles = width // LANES
    rim_rows = node_rows // 4
    chunk = node_rows // 5
    slots = geo * SLOTS
    place = jnp.arange(node_rows * DEGREE, dtype=jnp.int32) // DEGREE % 2
    index = edge_senders * tiles + PAD - tiles * place
    vmem = pl.BlockSpec(memory_space=pltpu.VMEM)
    smem = pl.BlockSpec(memory_space=pltpu.SMEM)
    hbm = pl.BlockSpec(memory_space=pl.ANY)
    dma = pltpu.SemaphoreType.DMA
    steps = pairs * SLOTS // STEP_ROWS
    return pl.pallas_call(
        functools.partial(kernel, bands, sectors),
        out_shape=jax.ShapeDtypeStruct((node_rows, width), BF16),
        in_specs=[vmem, vmem, smem, smem] + [vmem] * 6 + [hbm] * 3 + [vmem] * 3,
        out_specs=hbm,
        scratch_shapes=[
            pltpu.VMEM((pairs, SLOTS, embed), BF16),
            pltpu.VMEM((2, pairs, SLOTS, embed), BF16),
            pltpu.VMEM((slots, width), BF16),
            pltpu.VMEM((node_rows, width), BF16),
            pltpu.VMEM((2, width, width), BF16),
            pltpu.VMEM((2, width, width), BF16),
            pltpu.VMEM((rim_rows, slots), BF16),
            pltpu.VMEM((2, node_rows, width), BF16),
            pltpu.VMEM((2 * PAD + (node_rows + 9 * rim_rows) * tiles, LANES), F32),
            pltpu.VMEM((node_rows * tiles, LANES), F32),
            pltpu.VMEM((rim_rows * tiles, LANES), BF16),
            pltpu.VMEM((9, rim_rows * tiles, LANES), BF16),
            pltpu.VMEM((node_rows * tiles, LANES), F32),
            pltpu.VMEM((5, chunk, LANES), F32),
            pltpu.VMEM((5, chunk, LANES), F32),
            pltpu.VMEM((node_rows, width), BF16),
            dma((4,)),
            dma((2,)),
            dma((2,)),
            dma((pairs,)),
            dma((pairs,)),
            dma((steps,)),
            dma((steps,)),
            dma((4,)),
            dma((4,)),
            dma((8,)),
            dma((8,)),
            dma((5,)),
            dma((5,)),
            dma((5,)),
        ],
        compiler_params=pltpu.CompilerParams(
            collective_id=0, has_side_effects=True, vmem_limit_bytes=56 * 2**20
        ),
        name="encode_and_pass",
    )(
        obs_owner.reshape(1, rows),
        obs_node.reshape(1, rows),
        obs_count,
        index,
        obs_features,
        obs_in_w,
        obs_in_b.reshape(1, -1),
        obs_out_w,
        enc_w,
        enc_b.reshape(1, -1),
        node_base,
        recv_w,
        send_w,
        edge_b.reshape(1, -1),
        channel_scale.reshape(1, -1),
        norm_gain.reshape(1, -1),
    )


def solution(mesh):
    in_specs = (
        P(("band", "sector"), None),
        P(("band", "sector"), None),
        P(("band", "sector")),
        P(("band", "sector")),
        P(("band", "sector")),
        P(),
        P(),
        P(),
        P(None, "chan"),
        P("chan"),
        P(("band", "sector"), "chan"),
        P("chan", None),
        P("chan", None),
        P("chan"),
        P("chan"),
        P("chan"),
    )
    out_specs = P(("band", "sector"), "chan")
    return jax.shard_map(local, mesh=mesh, in_specs=in_specs, out_specs=out_specs, check_vma=False)
```

time: 244 us -> 90 us (0.37)
  Pallas kernels: 0 us -> 85.3 us
  waiting for transfers between devices: 84.4 us -> 0 us
  local copies, waits for them, and re-layouts: 59 us -> 2.46 us
  starting transfers between devices: 37.3 us -> 0 us
  other arithmetic: 29.6 us -> 1.4 us
  matrix products: 14.1 us -> 0 us
  between operations: 14.4 us -> 0.66 us
  blocking collectives: 3.92 us -> 0 us
    pallas_call x0 -> x1, Pallas kernels: none -> 85.3 us  [local(): pl.pallas_call(functools.partial(kernel, bands, sectors), out_shape=jax.S...]
    all_to_all x2 -> x0, waiting for transfers between devices: 50 us -> none  [the longest x1 49.9 us: local(): lax.all_to_all(payload.reshape(owner_total, capacity, -1), ('band', 'sect...]
    all_to_all x2 -> x0, starting transfers between devices: 29.5 us -> none  [the longest x1 16.3 us: local(): lax.all_to_all(slot_ids.reshape(owner_total, capacity), ('band', 'sector'...]
    gather x1 -> x0, local copies, waits for them, and re-layouts: 25.3 us -> none  [local(): table[edge_senders].astype(jnp.float32)]
    ppermute x4 -> x0, waiting for transfers between devices: 21.4 us -> none  [the longest x2 21.4 us: with_halo(): lax.ppermute(lax.slice_in_dim(block, block.shape[dim] - width, None, axis...]
    reduce_sum x4 -> x0, other arithmetic: 14.8 us -> none  [the longest x1 13.3 us: local(): agg = jnp.sum(jax.nn.silu(sender_rows + base[:, None, :]), axis=1)]
    convert_element_type x1 -> x0, local copies, waits for them, and re-layouts: 14.7 us -> none  [local(): table[edge_senders].astype(jnp.float32)]
    dot_general x5 -> x0, matrix products: 14.1 us -> none  [the longest x1 4.13 us: local(): node_sum = jnp.dot(picks, arrived, preferred_element_type=jnp.float32)]
  transfers between devices with their start and end apart: 8 -> 0, of which waited for: 6 -> 0; matrix products, arithmetic and copies ran while one was open for 9% -> 0% of each run, Pallas kernels for 0% -> 0%
where the time goes in v1:
time: 90 us; the launch traced here: 89.8 us
  Pallas kernels  85.3 us (95%)
  local copies, waits for them, and re-layouts  2.46 us (3%)
  other arithmetic  1.4 us (2%)
    pallas_call x1, Pallas kernels, local(): pl.pallas_call(functools.partial(kernel, bands, sectors), out_shape=jax.S...  85.3 us
    unnamed x1, local copies, waits for them, and re-layouts  2.46 us

profile of v1, /device:TPU:1, one launch (start us, length us, event | category | flops | bytes accessed | tf_op | source)
XLA Modules:
  0.0 89.8 jit_solution(10622568062551397451)
XLA Ops:
  0.7 1.4 %fusion.2.index_ref = s32[7680]{0:T(1024)} fusion(s32[7680]{0:T(1024)} %param.20), kind=kLoop, calls=%fused_computation.9 | loop fusion | flops 176640 | bytes 61440 | tf_op jit(solution)/shard_map/sub | solution.py:506
  2.1 85.3 %encode_and_pass.1 = bf16[1280,512]{1,0:T(8,128)(2,1)} custom-call(s32[1,1024]{1,0:T(1,128)} %bitcast.7, s32[1,1024]{1,0:T(1,128)} %bitcast.8, s32[1]{0:T(128)S(6)} %copy.18.count_ref, s32[7680]{0:T(1024)} %fusion.2.index_ref, bf16[1024,256]{1,0:T(8,128)(2,1)} %obs_ref.1, bf16[256,256]{1,0:T(8,128)(2,1)} %in_w_ref.1, f32[1,256]{1,0:T(1,128)} %bitcast.13, ...), custom_call_target="tpu_custom_call" | custom-call | tf_op jit(solution)/shard_map/encode_and_pass/pallas_call | solution.py:512
  87.3 2.5 %copy.19 = bf16[1280,512]{1,0:T(8,128)(2,1)} copy(bf16[1280,512]{1,0:T(8,128)(2,1)} %encode_and_pass.1) | data formatting | bytes 2621440

commit v2 on v1

--- a/solution.py
+++ b/solution.py
@@ -338,25 +338,60 @@
     project_send(0)
     rim[...] = table[pl.ds(PAD, rim_rows * tiles), :].astype(BF16)
 
-    def halo_copy(n):
-        i, j = around[n]
+    half_rows = rim_rows * tiles // 2
+    sides = [(0, 1), (0, -1), (1, 0), (-1, 0)]
+    turns = [(d, e) for d in sides for e in sides if (d[0] == 0) != (e[0] == 0)]
+
+    def group_of(i, j):
+        return (1 - i) * 3 + 1 - j
+
+    def half_of(n):
+        return pl.ds(n * half_rows, half_rows)
+
+    def halo_copy(half, d):
+        n = half * 4 + sides.index(d)
         return pltpu.make_async_remote_copy(
-            src_ref=rim,
-            dst_ref=halo.at[(1 - i) * 3 + 1 - j],
+            src_ref=rim.at[half_of(half)],
+            dst_ref=halo.at[group_of(*d), half_of(half)],
             send_sem=halo_sem.at[n],
             recv_sem=halo_in_sem.at[n],
-            device_id=neighbour(i, j),
+            device_id=neighbour(*d),
             device_id_type=MESH,
         )
 
-    for n in range(len(around)):
-        halo_copy(n).start()
+    def corner_copy(d, e):
+        half = 0 if d[0] == 0 else 1
+        n = 8 + turns.index((d, e))
+        return pltpu.make_async_remote_copy(
+            src_ref=halo.at[group_of(*d), half_of(half)],
+            dst_ref=halo.at[group_of(d[0] + e[0], d[1] + e[1]), half_of(half)],
+            send_sem=halo_sem.at[n],
+            recv_sem=halo_in_sem.at[n],
+            device_id=neighbour(*e),
+            device_id_type=MESH,
+        )
+
+    def widen(group, half):
+        first = PAD + (node_rows + group * rim_rows) * tiles + half * half_rows
+        table[pl.ds(first, half_rows), :] = halo[group, half_of(half)].astype(F32)
+
+    for first in (True, False):
+        for d in sides:
+            halo_copy(0 if (d[0] == 0) == first else 1, d).start()
+
+    make_latent(1)
+    for d in sides:
+        half = 0 if d[0] == 0 else 1
+        halo_copy(half, d).wait_recv()
+        for e in sides:
+            if (d, e) in turns:
+                corner_copy(d, e).start()
 
     def later_latent(q, carry):
         make_latent(q)
         return carry
 
-    lax.fori_loop(1, 4, later_latent, 0)
+    lax.fori_loop(2, 4, later_latent, 0)
     local[0].wait()
     weights[1].wait_recv()
     project_recv(0)
@@ -369,11 +404,14 @@
 
     lax.fori_loop(1, 4, later_project, 0)
 
-    for n, (i, j) in enumerate(around):
-        halo_copy(n).wait_recv()
-        group = (1 - i) * 3 + 1 - j
-        first = PAD + (node_rows + group * rim_rows) * tiles
-        table[pl.ds(first, rim_rows * tiles), :] = halo[group].astype(F32)
+    for d in sides:
+        half = 0 if d[0] == 0 else 1
+        widen(group_of(*d), half)
+        halo_copy(1 - half, d).wait_recv()
+        widen(group_of(*d), 1 - half)
+    for d, e in turns:
+        corner_copy(d, e).wait_recv()
+        widen(group_of(d[0] + e[0], d[1] + e[1]), 0 if d[0] == 0 else 1)
 
     upper = iota((2 * tiles, LANES), 0) < tiles
 
@@ -467,8 +505,11 @@
         copy.wait_send()
     for q in range(4):
         latent_copy(q, core).wait_send()
-    for n in range(len(around)):
-        halo_copy(n).wait_send()
+    for d in sides:
+        halo_copy(0, d).wait_send()
+        halo_copy(1, d).wait_send()
+    for d, e in turns:
+        corner_copy(d, e).wait_send()
     for n in range(chunks):
         part_copy(n).wait_send()
         out_copy(n).wait()
@@ -540,8 +581,8 @@
             dma((steps,)),
             dma((4,)),
             dma((4,)),
-            dma((8,)),
-            dma((8,)),
+            dma((16,)),
+            dma((16,)),
             dma((5,)),
             dma((5,)),
             dma((5,)),

time: 90 us -> 70.7 us (0.79)
  Pallas kernels: 85.3 us -> 66 us
    pallas_call x1, Pallas kernels: 85.3 us -> 66 us  [local(): pl.pallas_call(functools.partial(kernel, bands, sectors), out_shape=jax.S...]
where the time goes in v2:
time: 70.7 us; the launch traced here: 70.5 us
  Pallas kernels  66 us (93%)
  local copies, waits for them, and re-layouts  2.46 us (3%)
  other arithmetic  1.4 us (2%)
    pallas_call x1, Pallas kernels, local(): pl.pallas_call(functools.partial(kernel, bands, sectors), out_shape=jax.S...  66 us
    unnamed x1, local copies, waits for them, and re-layouts  2.46 us

profile of v2, /device:TPU:1, one launch (start us, length us, event | category | flops | bytes accessed | tf_op | source)
XLA Modules:
  0.0 70.5 jit_solution(16183655044697574360)
XLA Ops:
  0.7 1.4 %fusion.2.index_ref = s32[7680]{0:T(1024)} fusion(s32[7680]{0:T(1024)} %param.20), kind=kLoop, calls=%fused_computation.9 | loop fusion | flops 176640 | bytes 61440 | tf_op jit(solution)/shard_map/sub | solution.py:547
  2.1 66.0 %encode_and_pass.1 = bf16[1280,512]{1,0:T(8,128)(2,1)} custom-call(s32[1,1024]{1,0:T(1,128)} %bitcast.7, s32[1,1024]{1,0:T(1,128)} %bitcast.8, s32[1]{0:T(128)S(6)} %copy.18.count_ref, s32[7680]{0:T(1024)} %fusion.2.index_ref, bf16[1024,256]{1,0:T(8,128)(2,1)} %obs_ref.1, bf16[256,256]{1,0:T(8,128)(2,1)} %in_w_ref.1, f32[1,256]{1,0:T(1,128)} %bitcast.13, ...), custom_call_target="tpu_custom_call" | custom-call | tf_op jit(solution)/shard_map/encode_and_pass/pallas_call | solution.py:553
  68.1 2.5 %copy.19 = bf16[1280,512]{1,0:T(8,128)(2,1)} copy(bf16[1280,512]{1,0:T(8,128)(2,1)} %encode_and_pass.1) | data formatting | bytes 2621440

commit v3 on v2

v3 whole, which is shorter than its diff:
```python
import functools

import jax
import jax.numpy as jnp
from jax import lax
from jax.experimental import pallas as pl
from jax.experimental.pallas import tpu as pltpu
from jax.sharding import PartitionSpec as P

PIECES = 8
DEGREE = 6
SLOTS = 16
ID_ROW = 12
GROUP = 8
LANES = 128
LOW = 64
SKEW = 4
PARTS = 4
STEPS = 4
MESH = pl.DeviceIdType.MESH
F32 = jnp.float32
BF16 = jnp.bfloat16


def dot(a, b):
    return jnp.dot(a, b, preferred_element_type=F32)


def iota(shape, axis):
    return lax.broadcasted_iota(jnp.int32, shape, axis)


def half_silu(h):
    return h + h * jnp.tanh(h)


def kernel(
    bands,
    sectors,
    owner_ref,
    node_ref,
    count_ref,
    sender_ref,
    in_b_ref,
    enc_b_ref,
    edge_b_ref,
    scale_ref,
    gain_ref,
    obs_hbm,
    in_w_hbm,
    out_w_hbm,
    enc_w_hbm,
    base_hbm,
    recv_hbm,
    send_hbm,
    out_hbm,
    obs_ref,
    in_w_ref,
    out_w_ref,
    enc_w_ref,
    vectors,
    send_buf,
    arrived,
    message,
    node_base,
    recv_w,
    send_w,
    picks,
    latent,
    latent_in,
    table,
    recv_base,
    sent,
    sent_in,
    halo,
    agg,
    out_buf,
    local_sem,
    weight_sem,
    weight_in_sem,
    send_sem,
    arrive_sem,
    pass_sem,
    pass_in_sem,
    latent_sem,
    latent_in_sem,
    sent_sem,
    sent_in_sem,
    halo_sem,
    halo_in_sem,
    share_sem,
    share_in_sem,
    out_sem,
    out_send_sem,
    out_in_sem,
):
    band = lax.axis_index("band")
    sector = lax.axis_index("sector")
    core = lax.axis_index("chan")
    other = 1 - core
    geo = bands * sectors
    columns = sectors // 2
    pairs = bands * columns
    partner = (band, sector, other)
    rows = obs_ref.shape[0]
    node_rows, width = node_base.shape
    tiles = 2 * width // LANES
    run = node_rows // PARTS
    mine_rows = run // 2
    piece = mine_rows // 2
    table_rows = table.shape[0] // tiles
    base_rows = recv_base.shape[0] // tiles
    groups = geo // GROUP
    per_step = pairs // STEPS

    def local_copy(n, source, target):
        return pltpu.make_async_copy(source, target, local_sem.at[n])

    first_copies = [
        local_copy(0, obs_hbm, obs_ref),
        local_copy(1, in_w_hbm, in_w_ref),
        local_copy(2, out_w_hbm, out_w_ref),
    ]
    enc_copy = local_copy(3, enc_w_hbm, enc_w_ref)
    base_copy = local_copy(4, base_hbm, node_base)
    send_w_copy = local_copy(5, send_hbm, send_w.at[core])
    recv_w_copy = local_copy(6, recv_hbm, recv_w.at[core])
    for copy in first_copies + [enc_copy, base_copy, send_w_copy, recv_w_copy]:
        copy.start()

    sides = [(0, 1), (0, -1), (1, 0), (-1, 0)]

    def neighbour(i, j):
        return (
            lax.rem(band + (i + bands), bands),
            lax.rem(sector + (j + sectors), sectors),
            core,
        )

    to_sector = [lax.rem(sector + (2 * n + core), sectors) for n in range(columns)]
    barrier = pltpu.get_barrier_semaphore()

    def greet(device):
        pl.semaphore_signal(barrier, inc=1, device_id=device, device_id_type=MESH)

    greet(partner)
    for d in sides:
        greet(neighbour(*d))
    for i in range(bands):
        to_band = lax.rem(band + i, bands)
        for n in range(columns):
            if i == 0 and n == 0:

                @pl.when(core == 1)
                def _():
                    greet((to_band, to_sector[0], core))

            else:
                greet((to_band, to_sector[n], core))

    for copy in first_copies:
        copy.wait()
    obs = obs_ref[...]
    hidden = half_silu(0.5 * (dot(obs, in_w_ref[...]) + in_b_ref[...])).astype(BF16)
    embedded = (obs.astype(F32) + dot(hidden, out_w_ref[...])).astype(BF16)
    owner = owner_ref[...]
    node = node_ref[...]
    live = iota((1, rows), 1) < count_ref[0] * (rows // PIECES)
    same = (owner == iota((geo, rows), 0)).astype(F32)
    span = rows // 4
    upto = (iota((span, span), 0) <= iota((span, span), 1)).astype(F32).astype(BF16)
    before = jnp.zeros((geo, 1), F32)
    ranks = []
    for n in range(4):
        some = same[:, n * span : (n + 1) * span]
        rank = dot(some.astype(BF16), upto) + before
        before = rank[:, span - 1 :]
        ranks.append(jnp.sum(rank * some, axis=0, keepdims=True))
    position = jnp.concatenate(ranks, axis=1).astype(jnp.int32) - 1
    further = (owner % sectors - sector + sectors) % sectors
    valid = jnp.logical_and(live, further % 2 == core)
    step = (owner // sectors - band + bands) % bands * columns + further // 2
    slot = jnp.where(valid, step * SLOTS + position, -1)
    lane = SLOTS * (step % GROUP) + position
    high = iota((2 * LANES, rows), 0) == lane
    low = iota((2 * LANES, rows), 0) == lane + LANES
    ids = jnp.where(
        high,
        (node // LOW + 1).astype(F32),
        jnp.where(low, (node % LOW).astype(F32), 0.0),
    ).astype(BF16)
    mine = (iota((pairs, rows), 0) == jnp.where(valid, step, -1)).astype(F32).astype(BF16)
    id_rows = lax.dot_general(
        mine, ids, (((1,), (1,)), ((), ())), preferred_element_type=F32
    ).astype(BF16)

    def block_copy(i, n):
        k = i * columns + n
        return pltpu.make_async_remote_copy(
            src_ref=send_buf.at[k],
            dst_ref=arrived.at[core, k],
            send_sem=send_sem.at[k // per_step],
            recv_sem=arrive_sem.at[k // per_step],
            device_id=(lax.rem(band + i, bands), to_sector[n], core),
            device_id_type=MESH,
        )

    def pack(g):
        first = g * per_step * SLOTS
        count = per_step * SLOTS
        place = (slot == first + iota((count, rows), 0)).astype(F32).astype(BF16)
        spread = first + iota((count, pairs), 0) == iota((count, pairs), 1) * SLOTS + ID_ROW
        block = dot(place, embedded) + dot(spread.astype(F32).astype(BF16), id_rows)
        send_buf[pl.ds(g * per_step, per_step)] = block.astype(BF16).reshape(per_step, SLOTS, -1)

    def send(g):
        for k in range(g * per_step, (g + 1) * per_step):
            i, n = k // columns, k % columns
            if k == 0:

                @pl.when(core == 1)
                def _():
                    block_copy(0, 0).start()

                @pl.when(core == 0)
                def _():
                    pltpu.make_async_copy(
                        send_buf.at[0], arrived.at[core, 0], arrive_sem.at[0]
                    ).start()

            else:
                block_copy(i, n).start()

    pack(0)
    pl.semaphore_wait(barrier, pairs - 1 + core + len(sides) + 1)
    send(0)
    for g in range(1, STEPS):
        pack(g)
        send(g)

    def weight_copy(n, source, target):
        return pltpu.make_async_remote_copy(
            src_ref=source,
            dst_ref=target,
            send_sem=weight_sem.at[n],
            recv_sem=weight_in_sem.at[n],
            device_id=partner,
            device_id_type=MESH,
        )

    weights = [
        weight_copy(0, send_hbm, send_w.at[core]),
        weight_copy(1, recv_hbm, recv_w.at[core]),
    ] + [
        weight_copy(2 + n, ref, vectors.at[n, core])
        for n, ref in enumerate((edge_b_ref, scale_ref, gain_ref))
    ]
    for copy in weights:
        copy.start()
    for n, ref in enumerate((edge_b_ref, scale_ref, gain_ref)):
        vectors[n, core] = ref[...]

    def blocks_of(g):
        return pl.ds(g * per_step, per_step)

    def pass_on(g, side):
        block = arrived.at[side, blocks_of(g)]
        return pltpu.make_async_remote_copy(
            src_ref=block,
            dst_ref=block,
            send_sem=pass_sem.at[g],
            recv_sem=pass_in_sem.at[g],
            device_id=partner,
            device_id_type=MESH,
        )

    def group_wait(g, first=0):
        span = pl.ds(g * per_step + first, per_step - first)
        return pltpu.make_async_remote_copy(
            src_ref=send_buf.at[span],
            dst_ref=arrived.at[core, span],
            send_sem=send_sem.at[g],
            recv_sem=arrive_sem.at[g],
            device_id=partner,
            device_id_type=MESH,
        )

    def encode(side, g):
        block = arrived[side, blocks_of(g)].reshape(per_step * SLOTS, -1)
        content = half_silu(0.5 * (dot(block, enc_w_ref[...]) + enc_b_ref[...])).astype(BF16)
        first = pl.multiple_of((side * pairs + g * per_step) * SLOTS, per_step * SLOTS)
        message[pl.ds(first, per_step * SLOTS), :] = content

    enc_copy.wait()
    for g in range(STEPS):
        group_wait(g).wait_recv()
        pass_on(g, core).start()
        encode(core, g)
    for g in range(STEPS):
        pass_on(g, other).wait_recv()
        encode(other, g)

    slots = geo * SLOTS
    at = iota((groups, slots), 1)
    chosen = jnp.logical_and(
        at // (GROUP * SLOTS) == iota((groups, slots), 0), at % SLOTS == ID_ROW
    )
    found = dot(chosen.astype(F32).astype(BF16), arrived[...].reshape(slots, -1))
    slot_ids = ((found[:, :LANES] - 1.0) * LOW + found[:, LANES:]).astype(jnp.int32)

    def latent_copy(q):
        return pltpu.make_async_remote_copy(
            src_ref=latent.at[q, other],
            dst_ref=latent_in.at[q],
            send_sem=latent_sem.at[q],
            recv_sem=latent_in_sem.at[q],
            device_id=partner,
            device_id_type=MESH,
        )

    def make_latent(q):
        names = iota((run, LANES), 0) + q * run
        count = jnp.zeros((run, LANES), F32)
        for g in range(groups):
            hit = (names == slot_ids[g : g + 1, :]).astype(F32)
            count = count + hit
            picks[:, g * LANES : (g + 1) * LANES] = hit.astype(BF16)
        total = dot(picks[...], message[...])
        scale = 1.0 / jnp.maximum(jnp.sum(count, axis=1, keepdims=True), 1.0)
        base = node_base[pl.ds(pl.multiple_of(q * run, run), run), :].astype(F32)
        latent[q] = (base + total * scale).astype(BF16).reshape(2, mine_rows, width)
        latent_copy(q).start()

    def project(q, weight):
        return dot(latent[q, core], weight[core]) + dot(latent_in[q], weight[other])

    def tile(t):
        return slice(t * LANES, (t + 1) * LANES)

    def sent_copy(q):
        return pltpu.make_async_remote_copy(
            src_ref=sent.at[q],
            dst_ref=sent_in.at[q],
            send_sem=sent_sem.at[q],
            recv_sem=sent_in_sem.at[q],
            device_id=partner,
            device_id_type=MESH,
        )

    def project_send(q):
        value = (0.5 * project(q, send_w)).astype(BF16)
        wide = value.astype(F32)
        for t in range(tiles):
            for h in range(2):
                sent[q, h, t] = value[h * piece : (h + 1) * piece, tile(t)]
            table[pl.ds(t * table_rows + q * run + core * mine_rows, mine_rows), :] = wide[
                :, tile(t)
            ]
        sent_copy(q).start()

    def project_recv(q):
        value = project(q, recv_w).astype(BF16).astype(F32)
        for t in range(tiles):
            bias = vectors[0, t // (tiles // 2), :, tile(t % (tiles // 2))]
            recv_base[pl.ds(t * base_rows + q * mine_rows, mine_rows), :] = 0.5 * (
                value[:, tile(t)] + bias
            )

    def widen(first, source):
        for t in range(tiles):
            table[pl.ds(t * table_rows + first, piece), :] = source[t].astype(F32)

    base_copy.wait()
    make_latent(0)
    send_w_copy.wait()
    weights[0].wait_recv()
    latent_copy(0).wait_recv()
    project_send(0)

    turns = [(d, e) for d in sides for e in sides if (d[0] == 0) != (e[0] == 0)]

    def group_of(i, j):
        return (1 - i) * 3 + 1 - j

    def halo_copy(half, d):
        n = half * 4 + sides.index(d)
        return pltpu.make_async_remote_copy(
            src_ref=sent.at[0, half],
            dst_ref=halo.at[group_of(*d), core, half],
            send_sem=halo_sem.at[n],
            recv_sem=halo_in_sem.at[n],
            device_id=neighbour(*d),
            device_id_type=MESH,
        )

    def corner_copy(d, e):
        half = 0 if d[0] == 0 else 1
        n = 8 + turns.index((d, e))
        return pltpu.make_async_remote_copy(
            src_ref=halo.at[group_of(*d), core, half],
            dst_ref=halo.at[group_of(d[0] + e[0], d[1] + e[1]), core, half],
            send_sem=halo_sem.at[n],
            recv_sem=halo_in_sem.at[n],
            device_id=neighbour(*e),
            device_id_type=MESH,
        )

    def share(group, half, side):
        block = halo.at[group, side, half]
        return pltpu.make_async_remote_copy(
            src_ref=block,
            dst_ref=block,
            send_sem=share_sem.at[group * 2 + half],
            recv_sem=share_in_sem.at[group * 2 + half],
            device_id=partner,
            device_id_type=MESH,
        )

    def widen_halo(group, half, side):
        widen(
            node_rows + group * run + half * piece + side * mine_rows,
            halo.at[group, side, half],
        )

    for first in (True, False):
        for d in sides:
            halo_copy(0 if (d[0] == 0) == first else 1, d).start()

    make_latent(1)
    for d in sides:
        half = 0 if d[0] == 0 else 1
        halo_copy(half, d).wait_recv()
        for e in sides:
            if (d, e) in turns:
                corner_copy(d, e).start()
        share(group_of(*d), half, core).start()

    def later_latent(q, carry):
        make_latent(q)
        return carry

    lax.fori_loop(2, PARTS, later_latent, 0)
    recv_w_copy.wait()
    for copy in weights[1:]:
        copy.wait_recv()
    project_recv(0)

    def later_project(q, carry):
        latent_copy(q).wait_recv()
        project_send(q)
        project_recv(q)
        return carry

    lax.fori_loop(1, PARTS, later_project, 0)

    def widen_sent(q, carry):
        sent_copy(q).wait_recv()
        for h in range(2):
            widen(q * run + h * piece + other * mine_rows, sent_in.at[q, h])
        return carry

    lax.fori_loop(0, PARTS, widen_sent, 0)

    straight = [(d, 0 if d[0] == 0 else 1) for d in sides]
    for d, half in straight:
        halo_copy(1 - half, d).wait_recv()
        share(group_of(*d), 1 - half, core).start()
        widen_halo(group_of(*d), half, core)
        widen_halo(group_of(*d), 1 - half, core)
    for d, half in straight:
        for h in (half, 1 - half):
            share(group_of(*d), h, other).wait_recv()
            widen_halo(group_of(*d), h, other)
    corners = [(group_of(d[0] + e[0], d[1] + e[1]), 0 if d[0] == 0 else 1) for d, e in turns]
    for n, (d, e) in enumerate(turns):
        corner_copy(d, e).wait_recv()
        share(*corners[n], core).start()
        widen_halo(*corners[n], core)
    for group, half in corners:
        share(group, half, other).wait_recv()
        widen_halo(group, half, other)

    unroll = 16

    def one_node(q, r):
        place = q * mine_rows + r
        base = recv_base[pl.ds(place, tiles, stride=base_rows), :]
        first = (q * run + core * mine_rows + r) * DEGREE
        total = None
        for k in range(DEGREE):
            sender = table[pl.ds(sender_ref[first + k], tiles, stride=table_rows), :]
            term = half_silu(base + sender)
            total = term if total is None else total + term
        agg[pl.ds(place, tiles, stride=base_rows), :] = total

    def out_rows(q):
        return out_hbm.at[pl.ds(pl.multiple_of(q * run + core * mine_rows, mine_rows), mine_rows)]

    def out_keep(q):
        return pltpu.make_async_copy(out_buf.at[q, core], out_rows(q), out_sem.at[q])

    def out_send(q):
        return pltpu.make_async_remote_copy(
            src_ref=out_buf.at[q, other],
            dst_ref=out_rows(q),
            send_sem=out_send_sem.at[q],
            recv_sem=out_in_sem.at[q],
            device_id=partner,
            device_id_type=MESH,
        )

    def edges(q, carry):
        def some(m, inner):
            for u in range(unroll):
                one_node(q, m * unroll + u)
            return inner

        lax.fori_loop(0, mine_rows // unroll, some, 0)

        def scaled(t):
            bias = vectors[1, t // (tiles // 2), :, tile(t % (tiles // 2))]
            return agg[pl.ds(t * base_rows + q * mine_rows, mine_rows), :] * bias

        square = jnp.zeros((mine_rows, LANES), F32)
        for t in range(tiles):
            value = scaled(t)
            square = square + value * value
        mean = jnp.sum(square, axis=1, keepdims=True) / (2 * width)
        factor = lax.rsqrt(mean + 1e-05)

        def finish(side, held):
            for t in range(tiles // 2):
                gain = vectors[2, side, :, tile(t)]
                normed = scaled(side * (tiles // 2) + t) * factor * gain
                out_buf[q, side, :, tile(t)] = (held[:, tile(t)].astype(F32) + normed).astype(
                    BF16
                )

        for side in range(2):

            @pl.when(core == side)
            def _():
                finish(side, latent[q, side])
                finish(1 - side, latent_in[q])

        out_send(q).start()
        out_keep(q).start()
        return carry

    lax.fori_loop(0, PARTS, edges, 0)

    @pl.when(core == 0)
    def _():
        group_wait(0, 1).wait_send()

    @pl.when(core == 1)
    def _():
        group_wait(0).wait_send()

    for g in range(1, STEPS):
        group_wait(g).wait_send()
    for g in range(STEPS):
        pass_on(g, core).wait_send()
    for copy in weights:
        copy.wait_send()
    for q in range(PARTS):
        latent_copy(q).wait_send()
        sent_copy(q).wait_send()
    for d in sides:
        halo_copy(0, d).wait_send()
        halo_copy(1, d).wait_send()
        for half in range(2):
            share(group_of(*d), half, core).wait_send()
    for n, (d, e) in enumerate(turns):
        corner_copy(d, e).wait_send()
        share(*corners[n], core).wait_send()
    for q in range(PARTS):
        out_keep(q).wait()
        out_send(q).wait()


def local(
    obs_features,
    obs_owner,
    obs_node,
    obs_count,
    edge_senders,
    obs_in_w,
    obs_in_b,
    obs_out_w,
    enc_w,
    enc_b,
    node_base,
    recv_w,
    send_w,
    edge_b,
    channel_scale,
    norm_gain,
):
    bands = lax.axis_size("band")
    sectors = lax.axis_size("sector")
    geo = bands * sectors
    pairs = geo // 2
    rows, embed = obs_features.shape
    node_rows, width = node_base.shape
    tiles = 2 * width // LANES
    run = node_rows // PARTS
    mine_rows = run // 2
    piece = mine_rows // 2
    slots = geo * SLOTS
    vmem = pl.BlockSpec(memory_space=pltpu.VMEM)
    smem = pl.BlockSpec(memory_space=pltpu.SMEM)
    hbm = pl.BlockSpec(memory_space=pl.ANY)
    dma = pltpu.SemaphoreType.DMA
    return pl.pallas_call(
        functools.partial(kernel, bands, sectors),
        out_shape=jax.ShapeDtypeStruct((node_rows, width), BF16),
        in_specs=[vmem, vmem, smem, smem] + [vmem] * 5 + [hbm] * 7,
        out_specs=hbm,
        scratch_shapes=[
            pltpu.VMEM((rows, embed), BF16),
            pltpu.VMEM((embed, embed), BF16),
            pltpu.VMEM((embed, embed), BF16),
            pltpu.VMEM((embed, width), BF16),
            pltpu.VMEM((3, 2, 1, width), F32),
            pltpu.VMEM((pairs, SLOTS, embed), BF16),
            pltpu.VMEM((2, pairs, SLOTS, embed), BF16),
            pltpu.VMEM((slots, width), BF16),
            pltpu.VMEM((node_rows, width), BF16),
            pltpu.VMEM((2, width, 2 * width), BF16),
            pltpu.VMEM((2, width, 2 * width), BF16),
            pltpu.VMEM((run, slots), BF16),
            pltpu.VMEM((PARTS, 2, mine_rows, width), BF16),
            pltpu.VMEM((PARTS, mine_rows, width), BF16),
            pltpu.VMEM((tiles * (node_rows + 9 * run + SKEW), LANES), F32),
            pltpu.VMEM((tiles * (PARTS * mine_rows + SKEW), LANES), F32),
            pltpu.VMEM((PARTS, 2, tiles, piece, LANES), BF16),
            pltpu.VMEM((PARTS, 2, tiles, piece, LANES), BF16),
            pltpu.VMEM((9, 2, 2, tiles, piece, LANES), BF16),
            pltpu.VMEM((tiles * (PARTS * mine_rows + SKEW), LANES), F32),
            pltpu.VMEM((PARTS, 2, mine_rows, width), BF16),
            dma((7,)),
            dma((5,)),
            dma((5,)),
            dma((STEPS,)),
            dma((STEPS,)),
            dma((STEPS,)),
            dma((STEPS,)),
            dma((PARTS,)),
            dma((PARTS,)),
            dma((PARTS,)),
            dma((PARTS,)),
            dma((16,)),
            dma((16,)),
            dma((18,)),
            dma((18,)),
            dma((PARTS,)),
            dma((PARTS,)),
            dma((PARTS,)),
        ],
        compiler_params=pltpu.CompilerParams(
            collective_id=0, has_side_effects=True, vmem_limit_bytes=58 * 2**20
        ),
        name="encode_and_pass",
    )(
        obs_owner.reshape(1, rows),
        obs_node.reshape(1, rows),
        obs_count,
        edge_senders,
        obs_in_b.reshape(1, -1),
        enc_b.reshape(1, -1),
        edge_b.reshape(1, -1),
        channel_scale.reshape(1, -1),
        norm_gain.reshape(1, -1),
        obs_features,
        obs_in_w,
        obs_out_w,
        enc_w,
        node_base,
        recv_w,
        send_w,
    )


def solution(mesh):
    in_specs = (
        P(("band", "sector"), None),
        P(("band", "sector"), None),
        P(("band", "sector")),
        P(("band", "sector")),
        P(("band", "sector")),
        P(),
        P(),
        P(),
        P(None, "chan"),
        P("chan"),
        P(("band", "sector"), "chan"),
        P("chan", None),
        P("chan", None),
        P("chan"),
        P("chan"),
        P("chan"),
    )
    out_specs = P(("band", "sector"), "chan")
    return jax.shard_map(local, mesh=mesh, in_specs=in_specs, out_specs=out_specs, check_vma=False)
```

time: 70.7 us -> 65.8 us (0.931)
  Pallas kernels: 66 us -> 62.5 us
  other arithmetic: 1.4 us -> 0 us
    pallas_call x1, Pallas kernels: 66 us -> 62.5 us  [local(): pl.pallas_call(functools.partial(kernel, bands, sectors), out_shape=jax.S...]
    sub x1 -> x0, other arithmetic: 1.4 us -> none  [local(): index = edge_senders * tiles + PAD - tiles * place]
where the time goes in v3:
time: 65.8 us; the launch traced here: 65.6 us
  Pallas kernels  62.5 us (95%)
  local copies, waits for them, and re-layouts  2.46 us (4%)
  between operations  0.66 us (1%)
    pallas_call x1, Pallas kernels, local(): pl.pallas_call(functools.partial(kernel, bands, sectors), out_shape=jax.S...  62.5 us
    unnamed x1, local copies, waits for them, and re-layouts  2.46 us

profile of v3, /device:TPU:1, one launch (start us, length us, event | category | flops | bytes accessed | tf_op | source)
XLA Modules:
  0.0 65.6 jit_solution(13889678567008925544)
XLA Ops:
  0.7 62.5 %encode_and_pass.1 = bf16[1280,512]{1,0:T(8,128)(2,1)} custom-call(s32[1,1024]{1,0:T(1,128)} %bitcast.7, s32[1,1024]{1,0:T(1,128)} %bitcast.8, s32[1]{0:T(128)S(6)} %copy.18.count_ref, s32[7680]{0:T(1024)} %sender_ref.1, f32[1,256]{1,0:T(1,128)} %bitcast.13, f32[1,512]{1,0:T(1,128)} %bitcast.9, f32[1,512]{1,0:T(1,128)} %bitcast.10, f32[1,512]{1,0:T(1,128)} %bitcast.11, ...), custom_call_target="tpu_custom_call" | custom-call | tf_op jit(solution)/shard_map/encode_and_pass/pallas_call | solution.py:615
  63.2 2.5 %copy.19 = bf16[1280,512]{1,0:T(8,128)(2,1)} copy(bf16[1280,512]{1,0:T(8,128)(2,1)} %encode_and_pass.1) | data formatting | bytes 2621440

commit v4 on v3

--- a/solution.py
+++ b/solution.py
@@ -17,6 +17,8 @@
 SKEW = 4
 PARTS = 4
 STEPS = 4
+SIDE = 4
+ORDER = (2, 1, 3, 0)
 MESH = pl.DeviceIdType.MESH
 F32 = jnp.float32
 BF16 = jnp.bfloat16
@@ -53,12 +55,15 @@
     base_hbm,
     recv_hbm,
     send_hbm,
-    out_hbm,
+    out_ref,
     obs_ref,
     in_w_ref,
     out_w_ref,
     enc_w_ref,
     vectors,
+    slot_ids,
+    rim_sum,
+    rim_count,
     send_buf,
     arrived,
     message,
@@ -90,7 +95,6 @@
     halo_in_sem,
     share_sem,
     share_in_sem,
-    out_sem,
     out_send_sem,
     out_in_sem,
 ):
@@ -99,8 +103,7 @@
     core = lax.axis_index("chan")
     other = 1 - core
     geo = bands * sectors
-    columns = sectors // 2
-    pairs = bands * columns
+    pairs = geo // 2
     partner = (band, sector, other)
     rows = obs_ref.shape[0]
     node_rows, width = node_base.shape
@@ -113,6 +116,40 @@
     groups = geo // GROUP
     per_step = pairs // STEPS
 
+    sides = [(0, 1), (1, 0), (0, -1), (-1, 0)]
+
+    def neighbour(i, j):
+        return (
+            lax.rem(band + (i + bands), bands),
+            lax.rem(sector + (j + sectors), sectors),
+            core,
+        )
+
+    row, column = lax.div(band, SIDE), lax.rem(band, SIDE)
+    to_row = [lax.rem(row + n, SIDE) * SIDE for n in range(SIDE)]
+    to_column = [lax.rem(column + n, SIDE) for n in range(SIDE)]
+    to_sector = [lax.rem(sector + (2 * n + core), sectors) for n in range(SIDE)]
+
+    def target_of(k):
+        n, i, j = ORDER[k // SIDE**2], ORDER[k // SIDE % SIDE], ORDER[k % SIDE]
+        return to_row[i] + to_column[j], to_sector[n], core
+
+    barrier = pltpu.get_barrier_semaphore()
+
+    def greet(device):
+        pl.semaphore_signal(barrier, inc=1, device_id=device, device_id_type=MESH)
+
+    for k in range(pairs - 1):
+        greet(target_of(k))
+
+    @pl.when(core == 1)
+    def _():
+        greet(target_of(pairs - 1))
+
+    greet(partner)
+    for d in sides:
+        greet(neighbour(*d))
+
     def local_copy(n, source, target):
         return pltpu.make_async_copy(source, target, local_sem.at[n])
 
@@ -127,36 +164,6 @@
     recv_w_copy = local_copy(6, recv_hbm, recv_w.at[core])
     for copy in first_copies + [enc_copy, base_copy, send_w_copy, recv_w_copy]:
         copy.start()
-
-    sides = [(0, 1), (0, -1), (1, 0), (-1, 0)]
-
-    def neighbour(i, j):
-        return (
-            lax.rem(band + (i + bands), bands),
-            lax.rem(sector + (j + sectors), sectors),
-            core,
-        )
-
-    to_sector = [lax.rem(sector + (2 * n + core), sectors) for n in range(columns)]
-    barrier = pltpu.get_barrier_semaphore()
-
-    def greet(device):
-        pl.semaphore_signal(barrier, inc=1, device_id=device, device_id_type=MESH)
-
-    greet(partner)
-    for d in sides:
-        greet(neighbour(*d))
-    for i in range(bands):
-        to_band = lax.rem(band + i, bands)
-        for n in range(columns):
-            if i == 0 and n == 0:
-
-                @pl.when(core == 1)
-                def _():
-                    greet((to_band, to_sector[0], core))
-
-            else:
-                greet((to_band, to_sector[n], core))
 
     for copy in first_copies:
         copy.wait()
@@ -179,7 +186,18 @@
     position = jnp.concatenate(ranks, axis=1).astype(jnp.int32) - 1
     further = (owner % sectors - sector + sectors) % sectors
     valid = jnp.logical_and(live, further % 2 == core)
-    step = (owner // sectors - band + bands) % bands * columns + further // 2
+    owner_band = owner // sectors
+
+    def place_of(distance):
+        return jnp.where(
+            distance == 2, 0, jnp.where(distance == 1, 1, jnp.where(distance == 3, 2, 3))
+        )
+
+    step = (
+        place_of(further // 2) * SIDE**2
+        + place_of((owner_band // SIDE - row + SIDE) % SIDE) * SIDE
+        + place_of((owner_band % SIDE - column + SIDE) % SIDE)
+    )
     slot = jnp.where(valid, step * SLOTS + position, -1)
     lane = SLOTS * (step % GROUP) + position
     high = iota((2 * LANES, rows), 0) == lane
@@ -194,14 +212,13 @@
         mine, ids, (((1,), (1,)), ((), ())), preferred_element_type=F32
     ).astype(BF16)
 
-    def block_copy(i, n):
-        k = i * columns + n
+    def block_copy(k):
         return pltpu.make_async_remote_copy(
             src_ref=send_buf.at[k],
             dst_ref=arrived.at[core, k],
             send_sem=send_sem.at[k // per_step],
             recv_sem=arrive_sem.at[k // per_step],
-            device_id=(lax.rem(band + i, bands), to_sector[n], core),
+            device_id=target_of(k),
             device_id_type=MESH,
         )
 
@@ -215,21 +232,19 @@
 
     def send(g):
         for k in range(g * per_step, (g + 1) * per_step):
-            i, n = k // columns, k % columns
-            if k == 0:
-
-                @pl.when(core == 1)
-                def _():
-                    block_copy(0, 0).start()
-
-                @pl.when(core == 0)
-                def _():
-                    pltpu.make_async_copy(
-                        send_buf.at[0], arrived.at[core, 0], arrive_sem.at[0]
-                    ).start()
-
-            else:
-                block_copy(i, n).start()
+            if k < pairs - 1:
+                block_copy(k).start()
+                continue
+
+            @pl.when(core == 1)
+            def _():
+                block_copy(k).start()
+
+            @pl.when(core == 0)
+            def _():
+                pltpu.make_async_copy(
+                    send_buf.at[k], arrived.at[core, k], arrive_sem.at[k // per_step]
+                ).start()
 
     pack(0)
     pl.semaphore_wait(barrier, pairs - 1 + core + len(sides) + 1)
@@ -274,8 +289,8 @@
             device_id_type=MESH,
         )
 
-    def group_wait(g, first=0):
-        span = pl.ds(g * per_step + first, per_step - first)
+    def group_wait(g, less=0):
+        span = pl.ds(g * per_step, per_step - less)
         return pltpu.make_async_remote_copy(
             src_ref=send_buf.at[span],
             dst_ref=arrived.at[core, span],
@@ -285,28 +300,45 @@
             device_id_type=MESH,
         )
 
-    def encode(side, g):
-        block = arrived[side, blocks_of(g)].reshape(per_step * SLOTS, -1)
+    count = per_step * SLOTS
+    id_groups = per_step // GROUP
+    at = iota((8, count), 1)
+    chosen = jnp.logical_and(at // (GROUP * SLOTS) == iota((8, count), 0), at % SLOTS == ID_ROW)
+    chosen = chosen.astype(F32).astype(BF16)
+
+    def hits(q, names):
+        return (iota((run, LANES), 0) + q * run == names).astype(F32)
+
+    def take(side, g):
+        block = arrived[side, blocks_of(g)].reshape(count, -1)
         content = half_silu(0.5 * (dot(block, enc_w_ref[...]) + enc_b_ref[...])).astype(BF16)
-        first = pl.multiple_of((side * pairs + g * per_step) * SLOTS, per_step * SLOTS)
-        message[pl.ds(first, per_step * SLOTS), :] = content
+        start = pl.multiple_of((side * pairs + g * per_step) * SLOTS, count)
+        message[pl.ds(start, count), :] = content
+        found = dot(chosen, block)
+        names = ((found[:, :LANES] - 1.0) * LOW + found[:, LANES:]).astype(jnp.int32)
+        slot_ids[side * STEPS + g] = names
+        some = [hits(0, names[n : n + 1, :]) for n in range(id_groups)]
+        value = dot(jnp.concatenate(some, axis=1).astype(BF16), content)
+        return value, sum(some[1:], some[0])
 
     enc_copy.wait()
-    for g in range(STEPS):
-        group_wait(g).wait_recv()
-        pass_on(g, core).start()
-        encode(core, g)
-    for g in range(STEPS):
-        pass_on(g, other).wait_recv()
-        encode(other, g)
-
-    slots = geo * SLOTS
-    at = iota((groups, slots), 1)
-    chosen = jnp.logical_and(
-        at // (GROUP * SLOTS) == iota((groups, slots), 0), at % SLOTS == ID_ROW
-    )
-    found = dot(chosen.astype(F32).astype(BF16), arrived[...].reshape(slots, -1))
-    slot_ids = ((found[:, :LANES] - 1.0) * LOW + found[:, LANES:]).astype(jnp.int32)
+    for g in range(STEPS + 1):
+        if g < STEPS:
+            group_wait(g).wait_recv()
+            pass_on(g, core).start()
+        if g > 0:
+            pass_on(g - 1, other).wait_recv()
+        taken = []
+        if g < STEPS:
+            taken.append(take(core, g))
+        if g > 0:
+            taken.append(take(other, g - 1))
+            taken.append((rim_sum[...], rim_count[...]))
+        value, number = taken[0]
+        for more in taken[1:]:
+            value, number = value + more[0], number + more[1]
+        rim_sum[...] = value
+        rim_count[...] = number
 
     def latent_copy(q):
         return pltpu.make_async_remote_copy(
@@ -318,21 +350,26 @@
             device_id_type=MESH,
         )
 
-    def make_latent(q):
-        names = iota((run, LANES), 0) + q * run
-        count = jnp.zeros((run, LANES), F32)
-        for g in range(groups):
-            hit = (names == slot_ids[g : g + 1, :]).astype(F32)
-            count = count + hit
-            picks[:, g * LANES : (g + 1) * LANES] = hit.astype(BF16)
-        total = dot(picks[...], message[...])
-        scale = 1.0 / jnp.maximum(jnp.sum(count, axis=1, keepdims=True), 1.0)
+    def end_latent(q, total, number):
+        scale = 1.0 / jnp.maximum(jnp.sum(number, axis=1, keepdims=True), 1.0)
         base = node_base[pl.ds(pl.multiple_of(q * run, run), run), :].astype(F32)
         latent[q] = (base + total * scale).astype(BF16).reshape(2, mine_rows, width)
         latent_copy(q).start()
 
-    def project(q, weight):
-        return dot(latent[q, core], weight[core]) + dot(latent_in[q], weight[other])
+    def make_latent(q):
+        number = jnp.zeros((run, LANES), F32)
+        for g in range(groups):
+            n = g % id_groups
+            hit = hits(q, slot_ids[g // id_groups, n : n + 1, :])
+            number = number + hit
+            picks[:, g * LANES : (g + 1) * LANES] = hit.astype(BF16)
+        end_latent(q, dot(picks[...], message[...]), number)
+
+    def project(q, weight, arrival=None):
+        own = dot(latent[q, core], weight[core])
+        if arrival is not None:
+            arrival()
+        return own + dot(latent_in[q], weight[other])
 
     def tile(t):
         return slice(t * LANES, (t + 1) * LANES)
@@ -347,8 +384,8 @@
             device_id_type=MESH,
         )
 
-    def project_send(q):
-        value = (0.5 * project(q, send_w)).astype(BF16)
+    def project_send(q, arrival=None):
+        value = (0.5 * project(q, send_w, arrival)).astype(BF16)
         wide = value.astype(F32)
         for t in range(tiles):
             for h in range(2):
@@ -370,12 +407,14 @@
         for t in range(tiles):
             table[pl.ds(t * table_rows + first, piece), :] = source[t].astype(F32)
 
+    def first_arrival():
+        weights[0].wait_recv()
+        latent_copy(0).wait_recv()
+
     base_copy.wait()
-    make_latent(0)
+    end_latent(0, rim_sum[...], rim_count[...])
     send_w_copy.wait()
-    weights[0].wait_recv()
-    latent_copy(0).wait_recv()
-    project_send(0)
+    project_send(0, first_arrival)
 
     turns = [(d, e) for d in sides for e in sides if (d[0] == 0) != (e[0] == 0)]
 
@@ -422,18 +461,48 @@
             halo.at[group, side, half],
         )
 
-    for first in (True, False):
-        for d in sides:
-            halo_copy(0 if (d[0] == 0) == first else 1, d).start()
+    early = {d: 0 if d[0] == 0 else 1 for d in sides}
+    first_turns, second_turns = turns[: len(sides)], turns[len(sides) :]
+
+    def corner_of(d, e):
+        return group_of(d[0] + e[0], d[1] + e[1]), early[d]
+
+    def comes(d):
+        return {1: band > 0, 0: None, -1: band < bands - 1}[d[0]]
+
+    def goes(d):
+        return comes((-d[0], 0))
+
+    def when(condition, act):
+        if condition is None:
+            act()
+        else:
+            pl.when(condition)(act)
+
+    def comes_corner(d, e):
+        return comes((d[0] + e[0], 0))
+
+    def goes_corner(d, e):
+        return comes(d) if d[0] else goes(e)
+
+    for d in sides:
+        when(goes(d), lambda: halo_copy(early[d], d).start())
 
     make_latent(1)
     for d in sides:
-        half = 0 if d[0] == 0 else 1
-        halo_copy(half, d).wait_recv()
-        for e in sides:
-            if (d, e) in turns:
-                corner_copy(d, e).start()
-        share(group_of(*d), half, core).start()
+
+        def second_half():
+            halo_copy(early[d], d).wait_send()
+            halo_copy(1 - early[d], d).start()
+
+        when(goes(d), second_half)
+    for d in sides:
+        when(comes(d), lambda: halo_copy(early[d], d).wait_recv())
+        for t in first_turns:
+            if t[0] == d:
+                when(goes_corner(*t), lambda: corner_copy(*t).start())
+    for d in sides:
+        when(comes(d), lambda: share(group_of(*d), early[d], core).start())
 
     def later_latent(q, carry):
         make_latent(q)
@@ -452,6 +521,13 @@
         return carry
 
     lax.fori_loop(1, PARTS, later_project, 0)
+    for e in sides:
+        for t in first_turns:
+            if t[1] == e:
+                when(goes_corner(*t), lambda: corner_copy(*t).wait_send())
+        for t in second_turns:
+            if t[1] == e:
+                when(goes_corner(*t), lambda: corner_copy(*t).start())
 
     def widen_sent(q, carry):
         sent_copy(q).wait_recv()
@@ -461,24 +537,54 @@
 
     lax.fori_loop(0, PARTS, widen_sent, 0)
 
-    straight = [(d, 0 if d[0] == 0 else 1) for d in sides]
-    for d, half in straight:
-        halo_copy(1 - half, d).wait_recv()
-        share(group_of(*d), 1 - half, core).start()
-        widen_halo(group_of(*d), half, core)
-        widen_halo(group_of(*d), 1 - half, core)
-    for d, half in straight:
-        for h in (half, 1 - half):
-            share(group_of(*d), h, other).wait_recv()
-            widen_halo(group_of(*d), h, other)
-    corners = [(group_of(d[0] + e[0], d[1] + e[1]), 0 if d[0] == 0 else 1) for d, e in turns]
-    for n, (d, e) in enumerate(turns):
-        corner_copy(d, e).wait_recv()
-        share(*corners[n], core).start()
-        widen_halo(*corners[n], core)
-    for group, half in corners:
+    def widen_both(group, half):
+        widen_halo(group, half, core)
         share(group, half, other).wait_recv()
         widen_halo(group, half, other)
+
+    for d in sides:
+        when(comes(d), lambda: widen_both(group_of(*d), early[d]))
+
+    @pl.when(core == 0)
+    def _():
+        group_wait(STEPS - 1, 1).wait_send()
+
+    @pl.when(core == 1)
+    def _():
+        group_wait(STEPS - 1).wait_send()
+
+    for g in range(STEPS - 1):
+        group_wait(g).wait_send()
+    for g in range(STEPS):
+        pass_on(g, core).wait_send()
+    for copy in weights:
+        copy.wait_send()
+    for q in range(PARTS):
+        latent_copy(q).wait_send()
+        sent_copy(q).wait_send()
+
+    for d in sides:
+
+        def second_arrival():
+            halo_copy(1 - early[d], d).wait_recv()
+            share(group_of(*d), 1 - early[d], core).start()
+
+        when(comes(d), second_arrival)
+
+    def corner_arrival(t):
+        corner_copy(*t).wait_recv()
+        share(*corner_of(*t), core).start()
+
+    for t in first_turns:
+        when(comes_corner(*t), lambda: corner_arrival(t))
+    for d in sides:
+        when(comes(d), lambda: widen_both(group_of(*d), 1 - early[d]))
+    for t in first_turns:
+        when(comes_corner(*t), lambda: widen_both(*corner_of(*t)))
+    for t in second_turns:
+        when(comes_corner(*t), lambda: corner_arrival(t))
+    for t in second_turns:
+        when(comes_corner(*t), lambda: widen_both(*corner_of(*t)))
 
     unroll = 16
 
@@ -494,15 +600,12 @@
         agg[pl.ds(place, tiles, stride=base_rows), :] = total
 
     def out_rows(q):
-        return out_hbm.at[pl.ds(pl.multiple_of(q * run + core * mine_rows, mine_rows), mine_rows)]
-
-    def out_keep(q):
-        return pltpu.make_async_copy(out_buf.at[q, core], out_rows(q), out_sem.at[q])
+        return pl.ds(pl.multiple_of(q * run + core * mine_rows, mine_rows), mine_rows)
 
     def out_send(q):
         return pltpu.make_async_remote_copy(
-            src_ref=out_buf.at[q, other],
-            dst_ref=out_rows(q),
+            src_ref=out_buf.at[q],
+            dst_ref=out_ref.at[out_rows(q)],
             send_sem=out_send_sem.at[q],
             recv_sem=out_in_sem.at[q],
             device_id=partner,
@@ -528,54 +631,36 @@
         mean = jnp.sum(square, axis=1, keepdims=True) / (2 * width)
         factor = lax.rsqrt(mean + 1e-05)
 
-        def finish(side, held):
+        def finish(side, held, target):
             for t in range(tiles // 2):
                 gain = vectors[2, side, :, tile(t)]
                 normed = scaled(side * (tiles // 2) + t) * factor * gain
-                out_buf[q, side, :, tile(t)] = (held[:, tile(t)].astype(F32) + normed).astype(
-                    BF16
-                )
+                target[:, tile(t)] = (held[:, tile(t)].astype(F32) + normed).astype(BF16)
 
         for side in range(2):
 
             @pl.when(core == side)
             def _():
-                finish(side, latent[q, side])
-                finish(1 - side, latent_in[q])
+                finish(1 - side, latent_in[q], out_buf.at[q])
+                finish(side, latent[q, side], out_ref.at[out_rows(q)])
 
         out_send(q).start()
-        out_keep(q).start()
         return carry
 
     lax.fori_loop(0, PARTS, edges, 0)
 
-    @pl.when(core == 0)
-    def _():
-        group_wait(0, 1).wait_send()
-
-    @pl.when(core == 1)
-    def _():
-        group_wait(0).wait_send()
-
-    for g in range(1, STEPS):
-        group_wait(g).wait_send()
-    for g in range(STEPS):
-        pass_on(g, core).wait_send()
-    for copy in weights:
-        copy.wait_send()
-    for q in range(PARTS):
-        latent_copy(q).wait_send()
-        sent_copy(q).wait_send()
-    for d in sides:
-        halo_copy(0, d).wait_send()
-        halo_copy(1, d).wait_send()
+    def drain_side(d):
         for half in range(2):
             share(group_of(*d), half, core).wait_send()
-    for n, (d, e) in enumerate(turns):
-        corner_copy(d, e).wait_send()
-        share(*corners[n], core).wait_send()
+
+    for d in sides:
+        when(goes(d), lambda: halo_copy(1 - early[d], d).wait_send())
+        when(comes(d), lambda: drain_side(d))
+    for t in second_turns:
+        when(goes_corner(*t), lambda: corner_copy(*t).wait_send())
+    for t in turns:
+        when(comes_corner(*t), lambda: share(*corner_of(*t), core).wait_send())
     for q in range(PARTS):
-        out_keep(q).wait()
         out_send(q).wait()
 
 
@@ -614,15 +699,18 @@
     dma = pltpu.SemaphoreType.DMA
     return pl.pallas_call(
         functools.partial(kernel, bands, sectors),
-        out_shape=jax.ShapeDtypeStruct((node_rows, width), BF16),
+        out_shape=pltpu.VMEM((node_rows, width), BF16),
         in_specs=[vmem, vmem, smem, smem] + [vmem] * 5 + [hbm] * 7,
-        out_specs=hbm,
+        out_specs=vmem,
         scratch_shapes=[
             pltpu.VMEM((rows, embed), BF16),
             pltpu.VMEM((embed, embed), BF16),
             pltpu.VMEM((embed, embed), BF16),
             pltpu.VMEM((embed, width), BF16),
             pltpu.VMEM((3, 2, 1, width), F32),
+            pltpu.VMEM((2 * STEPS, 8, LANES), jnp.int32),
+            pltpu.VMEM((run, width), F32),
+            pltpu.VMEM((run, LANES), F32),
             pltpu.VMEM((pairs, SLOTS, embed), BF16),
             pltpu.VMEM((2, pairs, SLOTS, embed), BF16),
             pltpu.VMEM((slots, width), BF16),
@@ -638,7 +726,7 @@
             pltpu.VMEM((PARTS, 2, tiles, piece, LANES), BF16),
             pltpu.VMEM((9, 2, 2, tiles, piece, LANES), BF16),
             pltpu.VMEM((tiles * (PARTS * mine_rows + SKEW), LANES), F32),
-            pltpu.VMEM((PARTS, 2, mine_rows, width), BF16),
+            pltpu.VMEM((PARTS, mine_rows, width), BF16),
             dma((7,)),
             dma((5,)),
             dma((5,)),
@@ -656,10 +744,9 @@
             dma((18,)),
             dma((PARTS,)),
             dma((PARTS,)),
-            dma((PARTS,)),
         ],
         compiler_params=pltpu.CompilerParams(
-            collective_id=0, has_side_effects=True, vmem_limit_bytes=58 * 2**20
+            collective_id=0, has_side_effects=True, vmem_limit_bytes=56 * 2**20
         ),
         name="encode_and_pass",
     )(

time: 65.8 us -> 62.5 us (0.950)
  Pallas kernels: 62.5 us -> 60.1 us
  local copies, waits for them, and re-layouts: 2.46 us -> 1.06 us
    pallas_call x1, Pallas kernels: 62.5 us -> 60.1 us  [local(): pl.pallas_call(functools.partial(kernel, bands, sectors), out_shape=pltpu...]
    unnamed x1, local copies, waits for them, and re-layouts: 2.46 us -> 1.06 us
where the time goes in v4:
time: 62.5 us; the launch traced here: 61.8 us
  Pallas kernels  60.1 us (96%)
  local copies, waits for them, and re-layouts  1.06 us (2%)
  between operations  0.66 us (1%)
    pallas_call x1, Pallas kernels, local(): pl.pallas_call(functools.partial(kernel, bands, sectors), out_shape=pltpu...  60.1 us

profile of v4, /device:TPU:1, one launch (start us, length us, event | category | flops | bytes accessed | tf_op | source)
XLA Modules:
  0.0 61.8 jit_solution(10640400157139682070)
XLA Ops:
  0.7 60.1 %encode_and_pass.1 = bf16[1280,512]{1,0:T(8,128)(2,1)S(1)} custom-call(s32[1,1024]{1,0:T(1,128)} %bitcast.7, s32[1,1024]{1,0:T(1,128)} %bitcast.8, s32[1]{0:T(128)S(6)} %copy.19.count_ref, s32[7680]{0:T(1024)} %sender_ref.1, f32[1,256]{1,0:T(1,128)} %bitcast.13, f32[1,512]{1,0:T(1,128)} %bitcast.9, f32[1,512]{1,0:T(1,128)} %bitcast.10, f32[1,512]{1,0:T(1,128)} %bitcast.11, ...), custom_call_target="tpu_custom_call" | custom-call | tf_op jit(solution)/shard_map/encode_and_pass/pallas_call | solution.py:700
  60.8 1.1 %copy.18 = bf16[1280,512]{1,0:T(8,128)(2,1)} copy(bf16[1280,512]{1,0:T(8,128)(2,1)S(1)} %encode_and_pass.1) | data formatting | bytes 2621440

commit v5 on v4

--- a/solution.py
+++ b/solution.py
@@ -39,15 +39,15 @@
 def kernel(
     bands,
     sectors,
-    owner_ref,
-    node_ref,
     count_ref,
-    sender_ref,
-    in_b_ref,
-    enc_b_ref,
-    edge_b_ref,
-    scale_ref,
-    gain_ref,
+    owner_hbm,
+    node_hbm,
+    sender_hbm,
+    in_b_hbm,
+    enc_b_hbm,
+    edge_b_hbm,
+    scale_hbm,
+    gain_hbm,
     obs_hbm,
     in_w_hbm,
     out_w_hbm,
@@ -56,6 +56,11 @@
     recv_hbm,
     send_hbm,
     out_ref,
+    owner_ref,
+    node_ref,
+    sender_ref,
+    in_b_ref,
+    enc_b_ref,
     obs_ref,
     in_w_ref,
     out_w_ref,
@@ -116,6 +121,29 @@
     groups = geo // GROUP
     per_step = pairs // STEPS
 
+    def local_copy(n, source, target):
+        return pltpu.make_async_copy(source, target, local_sem.at[n])
+
+    first_copies = [
+        local_copy(0, obs_hbm, obs_ref),
+        local_copy(1, in_w_hbm, in_w_ref),
+        local_copy(2, out_w_hbm, out_w_ref),
+        local_copy(7, owner_hbm, owner_ref),
+        local_copy(8, node_hbm, node_ref),
+        local_copy(9, in_b_hbm, in_b_ref),
+    ]
+    sender_copy = local_copy(10, sender_hbm, sender_ref)
+    enc_copies = [local_copy(3, enc_w_hbm, enc_w_ref), local_copy(11, enc_b_hbm, enc_b_ref)]
+    vector_copies = [
+        local_copy(12 + n, ref, vectors.at[n, core])
+        for n, ref in enumerate((edge_b_hbm, scale_hbm, gain_hbm))
+    ]
+    base_copy = local_copy(4, base_hbm, node_base)
+    send_w_copy = local_copy(5, send_hbm, send_w.at[core])
+    recv_w_copy = local_copy(6, recv_hbm, recv_w.at[core])
+    for copy in first_copies:
+        copy.start()
+
     sides = [(0, 1), (1, 0), (0, -1), (-1, 0)]
 
     def neighbour(i, j):
@@ -150,23 +178,10 @@
     for d in sides:
         greet(neighbour(*d))
 
-    def local_copy(n, source, target):
-        return pltpu.make_async_copy(source, target, local_sem.at[n])
-
-    first_copies = [
-        local_copy(0, obs_hbm, obs_ref),
-        local_copy(1, in_w_hbm, in_w_ref),
-        local_copy(2, out_w_hbm, out_w_ref),
-    ]
-    enc_copy = local_copy(3, enc_w_hbm, enc_w_ref)
-    base_copy = local_copy(4, base_hbm, node_base)
-    send_w_copy = local_copy(5, send_hbm, send_w.at[core])
-    recv_w_copy = local_copy(6, recv_hbm, recv_w.at[core])
-    for copy in first_copies + [enc_copy, base_copy, send_w_copy, recv_w_copy]:
-        copy.start()
-
     for copy in first_copies:
         copy.wait()
+    for copy in enc_copies + [base_copy, send_w_copy, recv_w_copy, sender_copy] + vector_copies:
+        copy.start()
     obs = obs_ref[...]
     hidden = half_silu(0.5 * (dot(obs, in_w_ref[...]) + in_b_ref[...])).astype(BF16)
     embedded = (obs.astype(F32) + dot(hidden, out_w_ref[...])).astype(BF16)
@@ -268,12 +283,10 @@
         weight_copy(1, recv_hbm, recv_w.at[core]),
     ] + [
         weight_copy(2 + n, ref, vectors.at[n, core])
-        for n, ref in enumerate((edge_b_ref, scale_ref, gain_ref))
+        for n, ref in enumerate((edge_b_hbm, scale_hbm, gain_hbm))
     ]
     for copy in weights:
         copy.start()
-    for n, ref in enumerate((edge_b_ref, scale_ref, gain_ref)):
-        vectors[n, core] = ref[...]
 
     def blocks_of(g):
         return pl.ds(g * per_step, per_step)
@@ -300,45 +313,37 @@
             device_id_type=MESH,
         )
 
-    count = per_step * SLOTS
-    id_groups = per_step // GROUP
-    at = iota((8, count), 1)
-    chosen = jnp.logical_and(at // (GROUP * SLOTS) == iota((8, count), 0), at % SLOTS == ID_ROW)
+    count = pairs * SLOTS
+    id_groups = pairs // GROUP
+    at = iota((id_groups, count), 1)
+    chosen = jnp.logical_and(
+        at // (GROUP * SLOTS) == iota((id_groups, count), 0), at % SLOTS == ID_ROW
+    )
     chosen = chosen.astype(F32).astype(BF16)
 
     def hits(q, names):
         return (iota((run, LANES), 0) + q * run == names).astype(F32)
 
-    def take(side, g):
-        block = arrived[side, blocks_of(g)].reshape(count, -1)
+    def take(side):
+        block = arrived[side].reshape(count, -1)
         content = half_silu(0.5 * (dot(block, enc_w_ref[...]) + enc_b_ref[...])).astype(BF16)
-        start = pl.multiple_of((side * pairs + g * per_step) * SLOTS, count)
-        message[pl.ds(start, count), :] = content
+        message[pl.ds(pl.multiple_of(side * count, count), count), :] = content
         found = dot(chosen, block)
         names = ((found[:, :LANES] - 1.0) * LOW + found[:, LANES:]).astype(jnp.int32)
-        slot_ids[side * STEPS + g] = names
+        slot_ids[side] = names
         some = [hits(0, names[n : n + 1, :]) for n in range(id_groups)]
         value = dot(jnp.concatenate(some, axis=1).astype(BF16), content)
         return value, sum(some[1:], some[0])
 
-    enc_copy.wait()
-    for g in range(STEPS + 1):
-        if g < STEPS:
-            group_wait(g).wait_recv()
-            pass_on(g, core).start()
-        if g > 0:
-            pass_on(g - 1, other).wait_recv()
-        taken = []
-        if g < STEPS:
-            taken.append(take(core, g))
-        if g > 0:
-            taken.append(take(other, g - 1))
-            taken.append((rim_sum[...], rim_count[...]))
-        value, number = taken[0]
-        for more in taken[1:]:
-            value, number = value + more[0], number + more[1]
-        rim_sum[...] = value
-        rim_count[...] = number
+    for copy in enc_copies:
+        copy.wait()
+    for g in range(STEPS):
+        group_wait(g).wait_recv()
+        pass_on(g, core).start()
+    rim_sum[...], rim_count[...] = take(core)
+    for g in range(STEPS):
+        pass_on(g, other).wait_recv()
+    rim_rest, rim_more = take(other)
 
     def latent_copy(q):
         return pltpu.make_async_remote_copy(
@@ -405,14 +410,14 @@
 
     def widen(first, source):
         for t in range(tiles):
-            table[pl.ds(t * table_rows + first, piece), :] = source[t].astype(F32)
+            table[pl.ds(t * table_rows + first, source.shape[1]), :] = source[t].astype(F32)
 
     def first_arrival():
         weights[0].wait_recv()
         latent_copy(0).wait_recv()
 
     base_copy.wait()
-    end_latent(0, rim_sum[...], rim_count[...])
+    end_latent(0, rim_sum[...] + rim_rest, rim_count[...] + rim_more)
     send_w_copy.wait()
     project_send(0, first_arrival)
 
@@ -432,34 +437,36 @@
             device_id_type=MESH,
         )
 
-    def corner_copy(d, e):
+    split = piece * 3 // 5
+    cuts = {None: pl.ds(0, piece), 0: pl.ds(0, split), 1: pl.ds(split, piece - split)}
+
+    def corner_copy(d, e, cut=None):
         half = 0 if d[0] == 0 else 1
-        n = 8 + turns.index((d, e))
-        return pltpu.make_async_remote_copy(
-            src_ref=halo.at[group_of(*d), core, half],
-            dst_ref=halo.at[group_of(d[0] + e[0], d[1] + e[1]), core, half],
+        n = 8 + turns.index((d, e)) + (8 if cut == 1 else 0)
+        return pltpu.make_async_remote_copy(
+            src_ref=halo.at[group_of(*d), core, half, :, cuts[cut]],
+            dst_ref=halo.at[group_of(d[0] + e[0], d[1] + e[1]), core, half, :, cuts[cut]],
             send_sem=halo_sem.at[n],
             recv_sem=halo_in_sem.at[n],
             device_id=neighbour(*e),
             device_id_type=MESH,
         )
 
-    def share(group, half, side):
-        block = halo.at[group, side, half]
+    def share(group, half, side, cut=None):
+        block = halo.at[group, side, half, :, cuts[cut]]
+        n = group * 2 + half + (18 if cut == 1 else 0)
         return pltpu.make_async_remote_copy(
             src_ref=block,
             dst_ref=block,
-            send_sem=share_sem.at[group * 2 + half],
-            recv_sem=share_in_sem.at[group * 2 + half],
+            send_sem=share_sem.at[n],
+            recv_sem=share_in_sem.at[n],
             device_id=partner,
             device_id_type=MESH,
         )
 
-    def widen_halo(group, half, side):
-        widen(
-            node_rows + group * run + half * piece + side * mine_rows,
-            halo.at[group, side, half],
-        )
+    def widen_halo(group, half, side, cut=None):
+        first = node_rows + group * run + half * piece + side * mine_rows
+        widen(first + (split if cut == 1 else 0), halo.at[group, side, half, :, cuts[cut]])
 
     early = {d: 0 if d[0] == 0 else 1 for d in sides}
     first_turns, second_turns = turns[: len(sides)], turns[len(sides) :]
@@ -509,7 +516,8 @@
         return carry
 
     lax.fori_loop(2, PARTS, later_latent, 0)
-    recv_w_copy.wait()
+    for copy in [recv_w_copy, sender_copy] + vector_copies:
+        copy.wait()
     for copy in weights[1:]:
         copy.wait_recv()
     project_recv(0)
@@ -525,9 +533,10 @@
         for t in first_turns:
             if t[1] == e:
                 when(goes_corner(*t), lambda: corner_copy(*t).wait_send())
-        for t in second_turns:
-            if t[1] == e:
-                when(goes_corner(*t), lambda: corner_copy(*t).start())
+        for cut in range(2):
+            for t in second_turns:
+                if t[1] == e:
+                    when(goes_corner(*t), lambda: corner_copy(*t, cut).start())
 
     def widen_sent(q, carry):
         sent_copy(q).wait_recv()
@@ -571,9 +580,9 @@
 
         when(comes(d), second_arrival)
 
-    def corner_arrival(t):
-        corner_copy(*t).wait_recv()
-        share(*corner_of(*t), core).start()
+    def corner_arrival(t, cut=None):
+        corner_copy(*t, cut).wait_recv()
+        share(*corner_of(*t), core, cut).start()
 
     for t in first_turns:
         when(comes_corner(*t), lambda: corner_arrival(t))
@@ -581,12 +590,21 @@
         when(comes(d), lambda: widen_both(group_of(*d), 1 - early[d]))
     for t in first_turns:
         when(comes_corner(*t), lambda: widen_both(*corner_of(*t)))
-    for t in second_turns:
-        when(comes_corner(*t), lambda: corner_arrival(t))
-    for t in second_turns:
-        when(comes_corner(*t), lambda: widen_both(*corner_of(*t)))
-
-    unroll = 16
+    for cut in range(2):
+        for t in second_turns:
+            when(comes_corner(*t), lambda: corner_arrival(t, cut))
+        for t in second_turns:
+            when(comes_corner(*t), lambda: widen_halo(*corner_of(*t), core, cut))
+
+    def widen_shared(t, cut):
+        share(*corner_of(*t), other, cut).wait_recv()
+        widen_halo(*corner_of(*t), other, cut)
+
+    for cut in range(2):
+        for t in second_turns:
+            when(comes_corner(*t), lambda: widen_shared(t, cut))
+
+    unroll = 32
 
     def one_node(q, r):
         place = q * mine_rows + r
@@ -642,9 +660,9 @@
             @pl.when(core == side)
             def _():
                 finish(1 - side, latent_in[q], out_buf.at[q])
+                out_send(q).start()
                 finish(side, latent[q, side], out_ref.at[out_rows(q)])
 
-        out_send(q).start()
         return carry
 
     lax.fori_loop(0, PARTS, edges, 0)
@@ -656,10 +674,12 @@
     for d in sides:
         when(goes(d), lambda: halo_copy(1 - early[d], d).wait_send())
         when(comes(d), lambda: drain_side(d))
-    for t in second_turns:
-        when(goes_corner(*t), lambda: corner_copy(*t).wait_send())
-    for t in turns:
+    for t in first_turns:
         when(comes_corner(*t), lambda: share(*corner_of(*t), core).wait_send())
+    for cut in range(2):
+        for t in second_turns:
+            when(goes_corner(*t), lambda: corner_copy(*t, cut).wait_send())
+            when(comes_corner(*t), lambda: share(*corner_of(*t), core, cut).wait_send())
     for q in range(PARTS):
         out_send(q).wait()
 
@@ -700,15 +720,20 @@
     return pl.pallas_call(
         functools.partial(kernel, bands, sectors),
         out_shape=pltpu.VMEM((node_rows, width), BF16),
-        in_specs=[vmem, vmem, smem, smem] + [vmem] * 5 + [hbm] * 7,
+        in_specs=[smem] + [hbm] * 15,
         out_specs=vmem,
         scratch_shapes=[
+            pltpu.VMEM((1, rows), jnp.int32),
+            pltpu.VMEM((1, rows), jnp.int32),
+            pltpu.SMEM((node_rows * DEGREE,), jnp.int32),
+            pltpu.VMEM((1, embed), F32),
+            pltpu.VMEM((1, width), F32),
             pltpu.VMEM((rows, embed), BF16),
             pltpu.VMEM((embed, embed), BF16),
             pltpu.VMEM((embed, embed), BF16),
             pltpu.VMEM((embed, width), BF16),
             pltpu.VMEM((3, 2, 1, width), F32),
-            pltpu.VMEM((2 * STEPS, 8, LANES), jnp.int32),
+            pltpu.VMEM((2, pairs // GROUP, LANES), jnp.int32),
             pltpu.VMEM((run, width), F32),
             pltpu.VMEM((run, LANES), F32),
             pltpu.VMEM((pairs, SLOTS, embed), BF16),
@@ -727,7 +752,7 @@
             pltpu.VMEM((9, 2, 2, tiles, piece, LANES), BF16),
             pltpu.VMEM((tiles * (PARTS * mine_rows + SKEW), LANES), F32),
             pltpu.VMEM((PARTS, mine_rows, width), BF16),
-            dma((7,)),
+            dma((15,)),
             dma((5,)),
             dma((5,)),
             dma((STEPS,)),
@@ -738,10 +763,10 @@
             dma((PARTS,)),
             dma((PARTS,)),
             dma((PARTS,)),
-            dma((16,)),
-            dma((16,)),
-            dma((18,)),
-            dma((18,)),
+            dma((24,)),
+            dma((24,)),
+            dma((36,)),
+            dma((36,)),
             dma((PARTS,)),
             dma((PARTS,)),
         ],
@@ -750,9 +775,9 @@
         ),
         name="encode_and_pass",
     )(
+        obs_count,
         obs_owner.reshape(1, rows),
         obs_node.reshape(1, rows),
-        obs_count,
         edge_senders,
         obs_in_b.reshape(1, -1),
         enc_b.reshape(1, -1),

time: 62.5 us -> 59.6 us (0.954)
  Pallas kernels: 60.1 us -> 57.3 us
    pallas_call x1, Pallas kernels: 60.1 us -> 57.3 us  [local(): pl.pallas_call(functools.partial(kernel, bands, sectors), out_shape=pltpu...]
where the time goes in v5:
time: 59.6 us; the launch traced here: 59 us
  Pallas kernels  57.3 us (96%)
  local copies, waits for them, and re-layouts  1.06 us (2%)
  between operations  0.66 us (1%)
    pallas_call x1, Pallas kernels, local(): pl.pallas_call(functools.partial(kernel, bands, sectors), out_shape=pltpu...  57.3 us

profile of v5, /device:TPU:1, one launch (start us, length us, event | category | flops | bytes accessed | tf_op | source)
XLA Modules:
  0.0 59.0 jit_solution(7619063007258557317)
XLA Ops:
  0.7 57.3 %encode_and_pass.1 = bf16[1280,512]{1,0:T(8,128)(2,1)S(1)} custom-call(s32[1]{0:T(128)S(6)} %copy.19.count_ref, s32[1,1024]{1,0:T(1,128)} %bitcast.7, s32[1,1024]{1,0:T(1,128)} %bitcast.8, s32[7680]{0:T(1024)} %sender_hbm.1, f32[1,256]{1,0:T(1,128)} %bitcast.13, f32[1,512]{1,0:T(1,128)} %bitcast.9, f32[1,512]{1,0:T(1,128)} %bitcast.10, f32[1,512]{1,0:T(1,128)} %bitcast.11, ...), custom_call_target="tpu_custom_call" | custom-call | tf_op jit(solution)/shard_map/encode_and_pass/pallas_call | solution.py:720
  58.0 1.1 %copy.18 = bf16[1280,512]{1,0:T(8,128)(2,1)} copy(bf16[1280,512]{1,0:T(8,128)(2,1)S(1)} %encode_and_pass.1) | data formatting | bytes 2621440

commit v6 on v5

--- a/solution.py
+++ b/solution.py
@@ -83,7 +83,8 @@
     sent,
     sent_in,
     halo,
-    agg,
+    agg_even,
+    agg_odd,
     out_buf,
     local_sem,
     weight_sem,
@@ -261,11 +262,10 @@
                     send_buf.at[k], arrived.at[core, k], arrive_sem.at[k // per_step]
                 ).start()
 
-    pack(0)
+    for g in range(STEPS):
+        pack(g)
     pl.semaphore_wait(barrier, pairs - 1 + core + len(sides) + 1)
-    send(0)
-    for g in range(1, STEPS):
-        pack(g)
+    for g in range(STEPS):
         send(g)
 
     def weight_copy(n, source, target):
@@ -605,17 +605,19 @@
             when(comes_corner(*t), lambda: widen_shared(t, cut))
 
     unroll = 32
+    agg = (agg_even, agg_odd)
+
+    agg_rows = agg[0].shape[0] // tiles
 
     def one_node(q, r):
-        place = q * mine_rows + r
-        base = recv_base[pl.ds(place, tiles, stride=base_rows), :]
+        base = recv_base[pl.ds(q * mine_rows + r, tiles, stride=base_rows), :]
         first = (q * run + core * mine_rows + r) * DEGREE
         total = None
         for k in range(DEGREE):
             sender = table[pl.ds(sender_ref[first + k], tiles, stride=table_rows), :]
             term = half_silu(base + sender)
             total = term if total is None else total + term
-        agg[pl.ds(place, tiles, stride=base_rows), :] = total
+        agg[q % 2][pl.ds(r, tiles, stride=agg_rows), :] = total
 
     def out_rows(q):
         return pl.ds(pl.multiple_of(q * run + core * mine_rows, mine_rows), mine_rows)
@@ -630,42 +632,43 @@
             device_id_type=MESH,
         )
 
-    def edges(q, carry):
-        def some(m, inner):
-            for u in range(unroll):
-                one_node(q, m * unroll + u)
-            return inner
-
-        lax.fori_loop(0, mine_rows // unroll, some, 0)
-
-        def scaled(t):
-            bias = vectors[1, t // (tiles // 2), :, tile(t % (tiles // 2))]
-            return agg[pl.ds(t * base_rows + q * mine_rows, mine_rows), :] * bias
-
-        square = jnp.zeros((mine_rows, LANES), F32)
-        for t in range(tiles):
-            value = scaled(t)
+    def finish(q, r, some, between=None):
+        def scaled(side, t):
+            value = agg[q % 2][pl.ds((side * (tiles // 2) + t) * agg_rows + r, some), :]
+            return value * vectors[1, side, :, tile(t)]
+
+        values = [(side, t, scaled(side, t)) for side in (other, core) for t in range(tiles // 2)]
+        square = values[0][2] * values[0][2]
+        for _, _, value in values[1:]:
             square = square + value * value
         mean = jnp.sum(square, axis=1, keepdims=True) / (2 * width)
         factor = lax.rsqrt(mean + 1e-05)
-
-        def finish(side, held, target):
-            for t in range(tiles // 2):
-                gain = vectors[2, side, :, tile(t)]
-                normed = scaled(side * (tiles // 2) + t) * factor * gain
-                target[:, tile(t)] = (held[:, tile(t)].astype(F32) + normed).astype(BF16)
-
-        for side in range(2):
-
-            @pl.when(core == side)
-            def _():
-                finish(1 - side, latent_in[q], out_buf.at[q])
-                out_send(q).start()
-                finish(side, latent[q, side], out_ref.at[out_rows(q)])
-
-        return carry
-
-    lax.fori_loop(0, PARTS, edges, 0)
+        span = pl.ds(pl.multiple_of(r, unroll), some)
+        start = pl.multiple_of(q * run + core * mine_rows + r, unroll)
+        for n, (side, t, value) in enumerate(values):
+            if n == tiles // 2 and between is not None:
+                between()
+            held = latent_in[q, span, tile(t)] if side is other else latent[q, core, span, tile(t)]
+            normed = value * factor * vectors[2, side, :, tile(t)]
+            result = (held.astype(F32) + normed).astype(BF16)
+            if side is other:
+                out_buf[q, span, tile(t)] = result
+            else:
+                out_ref[pl.ds(start, some), tile(t)] = result
+
+    for q in range(PARTS):
+
+        def some_nodes(m, carry):
+            for u in range(unroll):
+                one_node(q, m * unroll + u)
+            if q > 0:
+                finish(q - 1, m * unroll, unroll)
+            return carry
+
+        lax.fori_loop(0, mine_rows // unroll, some_nodes, 0)
+        if q > 0:
+            out_send(q - 1).start()
+    finish(PARTS - 1, 0, mine_rows, lambda: out_send(PARTS - 1).start())
 
     def drain_side(d):
         for half in range(2):
@@ -750,7 +753,8 @@
             pltpu.VMEM((PARTS, 2, tiles, piece, LANES), BF16),
             pltpu.VMEM((PARTS, 2, tiles, piece, LANES), BF16),
             pltpu.VMEM((9, 2, 2, tiles, piece, LANES), BF16),
-            pltpu.VMEM((tiles * (PARTS * mine_rows + SKEW), LANES), F32),
+            pltpu.VMEM((tiles * (mine_rows + SKEW), LANES), F32),
+            pltpu.VMEM((tiles * (mine_rows + SKEW), LANES), F32),
             pltpu.VMEM((PARTS, mine_rows, width), BF16),
             dma((15,)),
             dma((5,)),

time: 59.6 us -> 58.7 us (0.985)
  Pallas kernels: 57.3 us -> 56.4 us
    pallas_call x1, Pallas kernels: 57.3 us -> 56.4 us  [local(): pl.pallas_call(functools.partial(kernel, bands, sectors), out_shape=pltpu...]
where the time goes in v6:
time: 58.7 us; the launch traced here: 58.1 us
  Pallas kernels  56.4 us (96%)
  local copies, waits for them, and re-layouts  1.06 us (2%)
  between operations  0.66 us (1%)
    pallas_call x1, Pallas kernels, local(): pl.pallas_call(functools.partial(kernel, bands, sectors), out_shape=pltpu...  56.4 us

profile of v6, /device:TPU:1, one launch (start us, length us, event | category | flops | bytes accessed | tf_op | source)
XLA Modules:
  0.0 58.1 jit_solution(15295564906336154107)
XLA Ops:
  0.7 56.4 %encode_and_pass.1 = bf16[1280,512]{1,0:T(8,128)(2,1)S(1)} custom-call(s32[1]{0:T(128)S(6)} %copy.19.count_ref, s32[1,1024]{1,0:T(1,128)} %bitcast.7, s32[1,1024]{1,0:T(1,128)} %bitcast.8, s32[7680]{0:T(1024)} %sender_hbm.1, f32[1,256]{1,0:T(1,128)} %bitcast.13, f32[1,512]{1,0:T(1,128)} %bitcast.9, f32[1,512]{1,0:T(1,128)} %bitcast.10, f32[1,512]{1,0:T(1,128)} %bitcast.11, ...), custom_call_target="tpu_custom_call" | custom-call | tf_op jit(solution)/shard_map/encode_and_pass/pallas_call | solution.py:723
  57.0 1.1 %copy.18 = bf16[1280,512]{1,0:T(8,128)(2,1)} copy(bf16[1280,512]{1,0:T(8,128)(2,1)S(1)} %encode_and_pass.1) | data formatting | bytes 2621440

commit v7 on v6

--- a/solution.py
+++ b/solution.py
@@ -511,6 +511,10 @@
     for d in sides:
         when(comes(d), lambda: share(group_of(*d), early[d], core).start())
 
+    for cut in range(2):
+        for t in second_turns:
+            when(goes_corner(*t), lambda: corner_copy(*t, cut).start())
+
     def later_latent(q, carry):
         make_latent(q)
         return carry
@@ -529,14 +533,8 @@
         return carry
 
     lax.fori_loop(1, PARTS, later_project, 0)
-    for e in sides:
-        for t in first_turns:
-            if t[1] == e:
-                when(goes_corner(*t), lambda: corner_copy(*t).wait_send())
-        for cut in range(2):
-            for t in second_turns:
-                if t[1] == e:
-                    when(goes_corner(*t), lambda: corner_copy(*t, cut).start())
+    for t in first_turns:
+        when(goes_corner(*t), lambda: corner_copy(*t).wait_send())
 
     def widen_sent(q, carry):
         sent_copy(q).wait_recv()

time: 58.7 us -> 57.1 us (0.973)
  Pallas kernels: 56.4 us -> 54.9 us
    pallas_call x1, Pallas kernels: 56.4 us -> 54.9 us  [local(): pl.pallas_call(functools.partial(kernel, bands, sectors), out_shape=pltpu...]
where the time goes in v7:
time: 57.1 us; the launch traced here: 56.6 us
  Pallas kernels  54.9 us (96%)
  local copies, waits for them, and re-layouts  1.06 us (2%)
  between operations  0.66 us (1%)
    pallas_call x1, Pallas kernels, local(): pl.pallas_call(functools.partial(kernel, bands, sectors), out_shape=pltpu...  54.9 us

profile of v7, /device:TPU:1, one launch (start us, length us, event | category | flops | bytes accessed | tf_op | source)
XLA Modules:
  0.0 56.6 jit_solution(7205459263865297158)
XLA Ops:
  0.7 54.9 %encode_and_pass.1 = bf16[1280,512]{1,0:T(8,128)(2,1)S(1)} custom-call(s32[1]{0:T(128)S(6)} %copy.19.count_ref, s32[1,1024]{1,0:T(1,128)} %bitcast.7, s32[1,1024]{1,0:T(1,128)} %bitcast.8, s32[7680]{0:T(1024)} %sender_hbm.1, f32[1,256]{1,0:T(1,128)} %bitcast.13, f32[1,512]{1,0:T(1,128)} %bitcast.9, f32[1,512]{1,0:T(1,128)} %bitcast.10, f32[1,512]{1,0:T(1,128)} %bitcast.11, ...), custom_call_target="tpu_custom_call" | custom-call | tf_op jit(solution)/shard_map/encode_and_pass/pallas_call | solution.py:721
  55.5 1.1 %copy.18 = bf16[1280,512]{1,0:T(8,128)(2,1)} copy(bf16[1280,512]{1,0:T(8,128)(2,1)S(1)} %encode_and_pass.1) | data formatting | bytes 2621440

commit v8 on v7

--- a/solution.py
+++ b/solution.py
@@ -508,12 +508,12 @@
         for t in first_turns:
             if t[0] == d:
                 when(goes_corner(*t), lambda: corner_copy(*t).start())
+        for cut in range(2):
+            for t in second_turns:
+                if t[0] == d:
+                    when(goes_corner(*t), lambda: corner_copy(*t, cut).start())
     for d in sides:
         when(comes(d), lambda: share(group_of(*d), early[d], core).start())
-
-    for cut in range(2):
-        for t in second_turns:
-            when(goes_corner(*t), lambda: corner_copy(*t, cut).start())
 
     def later_latent(q, carry):
         make_latent(q)

time: 57.1 us -> 57.1 us (level)
  no operation moved by 1% of the time
where the time goes in v8:
time: 57.1 us; the launch traced here: 56.6 us
  Pallas kernels  54.9 us (96%)
  local copies, waits for them, and re-layouts  1.06 us (2%)
  between operations  0.66 us (1%)
    pallas_call x1, Pallas kernels, local(): pl.pallas_call(functools.partial(kernel, bands, sectors), out_shape=pltpu...  54.9 us

profile of v8, /device:TPU:1, one launch (start us, length us, event | category | flops | bytes accessed | tf_op | source)
XLA Modules:
  0.0 56.6 jit_solution(10896048434987922328)
XLA Ops:
  0.7 54.9 %encode_and_pass.1 = bf16[1280,512]{1,0:T(8,128)(2,1)S(1)} custom-call(s32[1]{0:T(128)S(6)} %copy.19.count_ref, s32[1,1024]{1,0:T(1,128)} %bitcast.7, s32[1,1024]{1,0:T(1,128)} %bitcast.8, s32[7680]{0:T(1024)} %sender_hbm.1, f32[1,256]{1,0:T(1,128)} %bitcast.13, f32[1,512]{1,0:T(1,128)} %bitcast.9, f32[1,512]{1,0:T(1,128)} %bitcast.10, f32[1,512]{1,0:T(1,128)} %bitcast.11, ...), custom_call_target="tpu_custom_call" | custom-call | tf_op jit(solution)/shard_map/encode_and_pass/pallas_call | solution.py:721
  55.5 1.1 %copy.18 = bf16[1280,512]{1,0:T(8,128)(2,1)} copy(bf16[1280,512]{1,0:T(8,128)(2,1)S(1)} %encode_and_pass.1) | data formatting | bytes 2621440
